TPU v7x, 128 devices: a whole 4x4x4 slice. The times are simulated.
128 devices in a mesh: dp: 8 (over y, core), tensor: 16 (over z, x).
Axes of the slice: x: 4, y: 4, z: 4, core: 2. Of those that a mesh axis runs over, the one named last changes fastest.
Arguments:
- x_rows: bfloat16 [16384, 8192], P(('dp', 'tensor')), may hold values from -30 to 30
- d_attn: bfloat16 [16384, 4096], P('dp', 'tensor'), may hold values from -36 to 36
- q_saved: bfloat16 [16384, 4096], P('dp', 'tensor'), may hold values from -60 to 60
- k_saved: bfloat16 [16384, 2048], P('dp', 'tensor'), may hold values from -5 to 5, as said below
- v_saved: bfloat16 [16384, 2048], P('dp', 'tensor'), may hold values from -5 to 5, as said below
- w_query: bfloat16 [8192, 4096], P(None, 'tensor'), may hold values from -0.0625 to 0.0625
- w_key: bfloat16 [8192, 2048], P(None, 'tensor'), may hold values from -0.055242717 to 0.055242717, as said below
- w_value: bfloat16 [8192, 2048], P(None, 'tensor'), may hold values from -0.055242717 to 0.055242717, as said below
- down_all: bfloat16 [4, 48, 8192], replicated, may hold values from -0.0625 to 0.0625
- up_query: bfloat16 [4, 16, 4096], P(None, None, 'tensor'), may hold values from -0.09375 to 0.09375
- up_kv: bfloat16 [4, 32, 2048], P(None, None, 'tensor'), may hold values from -0.15625 to 0.15625, as said below
- tenant: int32 [16], P('dp'), may hold values from 0 to 3
- doc_starts: int32 [16, 4], P('dp'), may hold values from 0 to 1023, as said below
Outputs:
- d_rows: bfloat16 [16384, 8192], P(('dp', 'tensor'))
- upd_down: float32 [4, 48, 8192], P(None, None, 'tensor')
- upd_query: float32 [4, 16, 4096], P(None, None, 'tensor')
- upd_kv: float32 [4, 32, 2048], P(None, None, 'tensor')
Inputs may be any that keep to these rules, and one draw needn't show every extreme that they name: `k_saved`: column block b of 128 holds key head floor(b / 2); the 2 blocks of a head are equal. `v_saved`: column block b of 128 holds value head floor(b / 2); the 2 blocks of a head are equal. `w_key`: column block b of 128 belongs to key head floor(b / 2); the 2 blocks of a head are equal. `w_value`: column block b of 128 belongs to value head floor(b / 2); the 2 blocks of a head are equal. `up_kv`: column block b of 128 belongs to head floor(b / 2); the 2 blocks of a head are equal. `doc_starts`: each row lists the first positions of exactly 4 documents of its sequence: it begins with 0 and rises strictly. In the first sequence the last document is its last token alone.
All inputs are finite; a program needn't handle non-finite values.
Results may differ from a plain program's by a relative error of at most 0.02.
Values may be sent and summed in bfloat16 or wider, within the bound.
A program may use at most 384 MiB of HBM per device.

v0:
```python
import jax
import jax.numpy as jnp
from jax import lax
from jax.sharding import PartitionSpec as P

HD = 128
ADAPTER_RANK = 16
TEN = 4
SEQ = 1024


ADAPTER_SCALING = 2.0
ROPE_BASE = 500000.0
NORM_EPS = 1e-06
MASKED = -1e30


def from_partner(value, axis, apart):
    mask = 2**apart
    pairs = [(source, source ^ mask) for source in range(lax.axis_size(axis))]
    return lax.ppermute(value, axis, pairs)


def doc_layout(starts):
    where_pos = jnp.arange(SEQ, dtype=jnp.int32)
    inside = starts[None, :] <= where_pos[:, None]
    doc_index = jnp.sum(inside.astype(jnp.int32), axis=1)
    begin = jnp.max(jnp.where(inside, starts[None, :], jnp.zeros_like(starts)[None, :]), axis=1)
    offset = (where_pos - begin).astype(jnp.float32)
    allowed = (doc_index[:, None] == doc_index[None, :]) & (
        where_pos[None, :] <= where_pos[:, None]
    )
    return (offset, allowed)


def rotary_tables(offset, width):
    half = width // 2
    freq = ROPE_BASE ** (-(2.0 * jnp.arange(half, dtype=jnp.float32)) / width)
    angle = offset[..., None] * freq
    return (jnp.cos(angle), jnp.sin(angle))


def unrotate(grad, cosine, sine):
    half = grad.shape[-1] // 2
    first = grad[..., :half]
    second = grad[..., half:]
    return jnp.concatenate(
        [first * cosine + second * sine, second * cosine - first * sine], axis=-1
    )


def attention_back(query, key_rows, value_rows, grad_out, allowed, cosine, sine):
    scale = query.shape[-1] ** (-0.5)
    scores = (
        jnp.einsum("sphe,ske->shpk", query, key_rows, preferred_element_type=jnp.float32) * scale
    )
    scores = jnp.where(allowed[:, None, :, :], scores, MASKED)
    top = jnp.max(scores, axis=-1, keepdims=True)
    expd = jnp.exp(scores - top)
    probs = expd / jnp.sum(expd, axis=-1, keepdims=True)
    probs_low = probs.astype(jnp.bfloat16)
    output = jnp.einsum("shpk,ske->sphe", probs_low, value_rows, preferred_element_type=jnp.float32)
    delta = jnp.sum(grad_out.astype(jnp.float32) * output, axis=-1)
    dprob = jnp.einsum("sphe,ske->shpk", grad_out, value_rows, preferred_element_type=jnp.float32)
    dscore = probs * (dprob - jnp.transpose(delta, (0, 2, 1))[..., None])
    dscore_low = dscore.astype(jnp.bfloat16)
    dquery = (
        jnp.einsum("shpk,ske->sphe", dscore_low, key_rows, preferred_element_type=jnp.float32)
        * scale
    )
    dkey = (
        jnp.einsum("shpk,sphe->ske", dscore_low, query, preferred_element_type=jnp.float32) * scale
    )
    dvalue = jnp.einsum("shpk,sphe->ske", probs_low, grad_out, preferred_element_type=jnp.float32)
    dquery = unrotate(dquery, cosine[:, :, None, :], sine[:, :, None, :])
    dkey = unrotate(dkey, cosine, sine)
    return (dquery.astype(jnp.bfloat16), dkey.astype(jnp.bfloat16), dvalue.astype(jnp.bfloat16))


def one_sequence(item):
    query, key_rows, value_rows, grad_out, allowed, cosine, sine = item
    result = attention_back(
        query[None],
        key_rows[None],
        value_rows[None],
        grad_out[None],
        allowed[None],
        cosine[None],
        sine[None],
    )
    return (result[0][0], result[1][0], result[2][0])


def per_device(
    x_rows,
    d_attn,
    q_saved,
    k_saved,
    v_saved,
    w_query,
    w_key,
    w_value,
    down_all,
    up_query,
    up_kv,
    tenant,
    doc_starts,
):
    rows = x_rows.shape[0]
    width = x_rows.shape[1]
    group_tokens = q_saved.shape[0]
    local_heads = q_saved.shape[1] // HD
    sequences = group_tokens // SEQ
    tensor_size = lax.axis_size("tensor")
    here = lax.axis_index("tensor")
    contract = (((1,), (1,)), ((), ()))
    tenant_ids = jnp.arange(TEN, dtype=jnp.int32)
    seq_hot = (tenant[:, None] == tenant_ids[None, :]).astype(jnp.float32)
    token_tenant_onehot = jnp.repeat(seq_hot, SEQ, axis=0)
    row_hot = lax.dynamic_slice_in_dim(token_tenant_onehot, here * rows, rows, 0)
    down_flat = down_all.reshape(TEN * 3 * ADAPTER_RANK, width)
    low_all = lax.dot_general(down_flat, x_rows, contract, preferred_element_type=jnp.float32)
    low_pick = jnp.sum(low_all.reshape(TEN, 3 * ADAPTER_RANK, rows) * row_hot.T[:, None, :], axis=0)
    low_rows = lax.all_gather(low_pick.astype(jnp.bfloat16), "tensor", axis=1, tiled=True)
    offsets, allowed = jax.vmap(doc_layout)(doc_starts)
    cosine, sine = rotary_tables(offsets, HD)
    dq_low, dk_low, dv_low = lax.map(
        one_sequence,
        (
            q_saved.reshape(sequences, SEQ, local_heads, HD),
            k_saved.reshape(sequences, SEQ, HD),
            v_saved.reshape(sequences, SEQ, HD),
            d_attn.reshape(sequences, SEQ, local_heads, HD),
            allowed,
            cosine,
            sine,
        ),
    )
    query_gradient_flat = dq_low.reshape(group_tokens, local_heads * HD)
    key_gradient_flat = dk_low.reshape(group_tokens, HD)
    value_gradient_flat = dv_low.reshape(group_tokens, HD)
    back_q = lax.dot_general(
        up_query.reshape(TEN * ADAPTER_RANK, -1),
        query_gradient_flat,
        contract,
        preferred_element_type=jnp.float32,
    )
    back_k = lax.dot_general(
        up_kv[:, :ADAPTER_RANK, :].reshape(TEN * ADAPTER_RANK, HD),
        key_gradient_flat,
        contract,
        preferred_element_type=jnp.float32,
    )
    back_v = lax.dot_general(
        up_kv[:, ADAPTER_RANK:, :].reshape(TEN * ADAPTER_RANK, HD),
        value_gradient_flat,
        contract,
        preferred_element_type=jnp.float32,
    )
    backward_every_tenant = jnp.concatenate(
        [
            back_q.reshape(TEN, ADAPTER_RANK, group_tokens),
            back_k.reshape(TEN, ADAPTER_RANK, group_tokens),
            back_v.reshape(TEN, ADAPTER_RANK, group_tokens),
        ],
        axis=1,
    )
    backward_chosen_tenant = ADAPTER_SCALING * jnp.sum(
        backward_every_tenant * token_tenant_onehot.T[:, None, :], axis=0
    )
    low_grad = lax.psum_scatter(
        backward_chosen_tenant.astype(jnp.bfloat16), "tensor", scatter_dimension=1, tiled=True
    ).astype(jnp.float32)
    masked_low = low_rows[None, :, :] * token_tenant_onehot.T[:, None, :].astype(jnp.bfloat16)
    query_gradient = ADAPTER_SCALING * jnp.dot(
        masked_low[:, :ADAPTER_RANK].reshape(TEN * ADAPTER_RANK, group_tokens),
        query_gradient_flat,
        preferred_element_type=jnp.float32,
    ).reshape(TEN, ADAPTER_RANK, -1)
    key_gradient = ADAPTER_SCALING * jnp.dot(
        masked_low[:, ADAPTER_RANK : 2 * ADAPTER_RANK].reshape(TEN * ADAPTER_RANK, group_tokens),
        key_gradient_flat,
        preferred_element_type=jnp.float32,
    ).reshape(TEN, ADAPTER_RANK, HD)
    value_gradient = ADAPTER_SCALING * jnp.dot(
        masked_low[:, 2 * ADAPTER_RANK :].reshape(TEN * ADAPTER_RANK, group_tokens),
        value_gradient_flat,
        preferred_element_type=jnp.float32,
    ).reshape(TEN, ADAPTER_RANK, HD)
    grad_kv = jnp.concatenate([key_gradient, value_gradient], axis=1)
    grad_kv = grad_kv + from_partner(grad_kv.astype(jnp.bfloat16), "tensor", 0).astype(
        grad_kv.dtype
    )
    total = lax.dot_general(
        query_gradient_flat, w_query, contract, preferred_element_type=jnp.float32
    )
    total = total + lax.dot_general(
        key_gradient_flat, w_key, contract, preferred_element_type=jnp.float32
    )
    frozen = lax.psum_scatter(
        (
            total
            + lax.dot_general(
                value_gradient_flat, w_value, contract, preferred_element_type=jnp.float32
            )
        ).astype(jnp.bfloat16),
        "tensor",
        scatter_dimension=0,
        tiled=True,
    ).astype(jnp.float32)
    spread = (row_hot[:, :, None] * low_grad.T[:, None, :]).reshape(rows, TEN * 3 * ADAPTER_RANK)
    down_wide = down_flat.astype(jnp.float32)
    lowrank_dx = jnp.dot(spread, down_wide, precision=lax.Precision.HIGHEST)
    d_rows = (frozen + lowrank_dx).astype(jnp.bfloat16)
    weighted = (row_hot.T[:, None, :] * low_grad[None, :, :]).reshape(TEN * 3 * ADAPTER_RANK, rows)
    down_part = jnp.dot(
        weighted, x_rows.astype(jnp.float32), precision=lax.Precision.HIGHEST
    ).reshape(TEN, 3 * ADAPTER_RANK, width)
    local_width = width // tensor_size
    down_whole = lax.psum(down_part, ("dp", "tensor"))
    down_grad = lax.dynamic_slice_in_dim(down_whole, here * local_width, local_width, 2)
    query_gradient, grad_kv = (
        lax.psum(query_gradient.astype(jnp.bfloat16), "dp").astype(jnp.float32),
        lax.psum(grad_kv.astype(jnp.bfloat16), "dp").astype(jnp.float32),
    )
    square_down = jnp.sum((down_grad * down_grad).reshape(TEN, 3, -1), axis=2)
    square_q = jnp.sum((query_gradient * query_gradient).reshape(TEN, -1), axis=1)
    square_kv = jnp.sum((grad_kv * grad_kv).reshape(TEN, 2, -1), axis=2)
    total_down, total_q, total_kv = lax.psum((square_down, square_q, square_kv), "tensor")
    count_down = ADAPTER_RANK * width
    count_q = ADAPTER_RANK * query_gradient.shape[2] * tensor_size
    count_kv = ADAPTER_RANK * HD * tensor_size
    upd_down = (
        down_grad.reshape(TEN, 3, ADAPTER_RANK, -1)
        / jnp.sqrt(total_down / count_down + NORM_EPS)[:, :, None, None]
    ).reshape(down_grad.shape)
    upd_query = query_gradient / jnp.sqrt(total_q / count_q + NORM_EPS)[:, None, None]
    upd_kv = (
        grad_kv.reshape(TEN, 2, ADAPTER_RANK, -1)
        / jnp.sqrt(total_kv / count_kv + NORM_EPS)[:, :, None, None]
    ).reshape(grad_kv.shape)
    return (d_rows, upd_down, upd_query, upd_kv)


def solution(mesh):
    in_specs = (
        P(("dp", "tensor"), None),
        P("dp", "tensor"),
        P("dp", "tensor"),
        P("dp", "tensor"),
        P("dp", "tensor"),
        P(None, "tensor"),
        P(None, "tensor"),
        P(None, "tensor"),
        P(),
        P(None, None, "tensor"),
        P(None, None, "tensor"),
        P("dp"),
        P("dp", None),
    )
    out_specs = (
        P(("dp", "tensor"), None),
        P(None, None, "tensor"),
        P(None, None, "tensor"),
        P(None, None, "tensor"),
    )
    return jax.shard_map(
        per_device, mesh=mesh, in_specs=in_specs, out_specs=out_specs, check_vma=False
    )
```

profile of v0, /device:TPU:0, one launch (start us, length us, event | category | flops | bytes accessed | tf_op | source)
XLA Modules:
  0.0 516.4 jit_solution(1274234066515702343)
XLA Ops:
  12.2 2.6 fusion.60
  14.7 27.1 %all_gather.3 = bf16[48,2048]{1,0:T(8,128)(2,1)} all-gather(bf16[48,128]{1,0:T(8,128)(2,1)S(1)} %fusion.60), channel_id=1, replica_groups=mesh['dp'=8,'tensor'=16] {'tensor'}, dimensions={1}, use_global_device_ids=true | all-gather | bytes 208896 | tf_op jit(solution)/shard_map/all_gather | solution.py:124
  41.9 2.2 reshape.247
  44.1 2.2 reshape.245
  46.2 2.8 multiply_sine_fusion
  49.0 3.7 compare_and_fusion
  52.7 68.1 %while.14 = (s32[]{:T(128)}, bf16[2,1024,2,128]{3,2,1,0:T(2,128)(2,1)}, bf16[2,1024,128]{2,1,0:T(8,128)(2,1)}, bf16[2,1024,128]{2,1,0:T(8,128)(2,1)}, bf16[2,102...) while((s32[]{:T(128)}, ...), condition=%wide.region_6.7_spmd, body=%wide.region_2.6_spmd.sunk | while | flops 3276007424 | bytes 98132360 | solution.py:127
  52.7 2.3 dynamic-slice_bitcast_fusion.4
  55.0 2.9 constant_dynamic-slice_fusion.4
  57.9 2.0 copy.107
  59.9 3.4 fusion.127
  65.4 3.1 fusion.129
  68.4 3.0 fusion.133
  71.4 3.6 fusion.130
  84.5 2.2 constant_dynamic-update-slice_fusion.4
  86.7 2.3 dynamic-slice_bitcast_fusion.4
  89.0 2.9 constant_dynamic-slice_fusion.4
  91.9 2.0 copy.107
  93.9 3.4 fusion.127
  99.4 3.1 fusion.129
  102.5 2.9 fusion.133
  105.4 3.6 fusion.130
  118.6 2.2 constant_dynamic-update-slice_fusion.4
  132.3 2.5 reshape.266
  134.8 25.9 %fusion.84 = f32[2048,8192]{1,0:T(8,128)} fusion(bf16[2048,128]{1,0:T(8,128)(2,1)} %bitcast.253, bf16[8192,128]{1,0:T(8,128)(2,1)} %param.21), kind=kOutput, calls=%fused_computation.117 | convolution fusion | flops 4294967296 | bytes 69730304 | tf_op jit(solution)/shard_map/dot_general | solution.py:197
  160.8 26.0 %fusion.85 = f32[2048,8192]{1,0:T(8,128)} fusion(bf16[2048,128]{1,0:T(8,128)(2,1)} %bitcast.32, bf16[8192,128]{1,0:T(8,128)(2,1)} %param.22), kind=kOutput, calls=%fused_computation.118 | convolution fusion | flops 4294967296 | bytes 69730304 | tf_op jit(solution)/shard_map/dot_general | solution.py:203
  189.4 14.9 %reduce-scatter.7.cloned.1.call-done = bf16[128,48]{1,0:T(8,128)(2,1)} async-done(((bf16[2048,48]{1,0:T(8,128)(2,1)}), bf16[128,48]{1,0:T(8,128)(2,1)}) %reduce-scatter.7.cloned.1.call-update) | async-done | bytes 12304
  205.2 6.8 %fusion.54 = f32[4,48,8192]{2,1,0:T(8,128)} fusion(bf16[128,8192]{1,0:T(8,128)(2,1)} %param.15, f32[48,128]{1,0:T(8,128)S(1)} %get-tuple-element.151, f32[4,128]{1,0:T(4,128)S(1)} %copy-done.13), kind=kOutput, calls=%fused_computation.62 | convolution fusion | flops 2415943680 | bytes 8415232 | tf_op jit(solution)/shard_map/dot_general | solution.py:216
  212.0 55.8 %add_convert_fusion.2 = bf16[2048,8192]{1,0:T(8,128)(2,1)} fusion(f32[2048,8192]{1,0:T(8,128)} %fusion.85, f32[2048,8192]{1,0:T(8,128)} %fusion.84, bf16[8192,256]{1,0:T(8,128)(2,1)} %param.20, bf16[256,8,2,128]{3,2,1,0:T(2,128)(2,1)} %bitcast.250), kind=kOutput, calls=%fused_computation.54 | convolution fusion | flops 8640266240 | bytes 173015040 | tf_op jit(solution)/shard_map/dot_general | solution.py:194
  269.8 188.1 %all-reduce.5.cloned.1.call-done = f32[4,48,8192]{2,1,0:T(8,128)} async-done(((f32[4,48,8192]{2,1,0:T(8,128)}), f32[4,48,8192]{2,1,0:T(8,128)}) %all-reduce.5.cloned.1.call-update) | async-done | bytes 6291472 | tf_op jit(solution)/shard_map/psum | solution.py:220
  459.2 39.7 %all-reduce = (f32[4,3]{1,0:T(4,128)S(1)}, f32[4]{0:T(128)S(1)}, f32[4,2]{1,0:T(4,128)S(1)}) all-reduce(f32[4,3]{1,0:T(4,128)S(1)} %reduce_sum.92, f32[4]{0:T(128)S(1)} %fusion.74, f32[4,2]{1,0:T(4,128)S(1)} %reduce_sum.97), channel_id=1, replica_groups=mesh['dp'=8,'tensor'=16] {'tensor'}, use_global_device_ids=true, to_apply=%region_13.14 | all-reduce | flops 24 | bytes 192 | tf_op jit(solution)/shard_map/psum | solution.py:229
  504.1 4.9 fusion.51
  (125 shorter events, 50.5 us)
Async XLA Ops:
  8.0 4.2 copy-start
  8.0 196.3 %reduce-scatter.7.cloned.1.call-start = ((), (), s32[]{:S(2)}) async-start(), calls=%async_computation.4 | async-start | bytes 557056
  11.0 41.7 %copy-start.10 = (f32[1,4,2,1024]{3,1,2,0:T(4,128)}, f32[1,4,2,1024]{3,1,2,0:T(4,128)S(1)}, u32[]{:S(2)}) copy-start(f32[1,4,2,1024]{3,1,2,0:T(4,128)S(1)} %copy.79) | copy-start | bytes 98308
  11.6 0.6 copy-start.12
  52.7 68.1 %copy-start.14 = (bf16[4,2048]{1,0:T(4,128)(2,1)S(1)}, bf16[4,2048]{1,0:T(4,128)(2,1)}, u32[]{:S(2)}) copy-start(bf16[4,2048]{1,0:T(4,128)(2,1)} %bitcast_convert_fusion) | copy-start | bytes 49156
  59.9 3.4 copy-start.1
  63.3 2.0 copy-start.4
  63.3 2.0 copy-start.15
  65.3 3.1 copy-start.3
  71.4 3.6 copy-start.2
  71.4 5.1 copy-start.8
  75.0 2.3 copy-start.5
  75.0 2.3 copy-start.6
  93.9 3.4 copy-start.1
  97.3 2.0 copy-start.4
  97.3 2.0 copy-start.15
  99.4 3.1 copy-start.3
  105.4 3.6 copy-start.2
  105.4 5.1 copy-start.8
  109.0 2.3 copy-start.5
  109.0 2.3 copy-start.6
  120.8 10.2 %copy-start.11 = (f32[1,4,2,1024]{3,1,2,0:T(4,128)S(1)}, f32[1,4,2,1024]{3,1,2,0:T(4,128)}, u32[]{:S(2)}) copy-start(f32[1,4,2,1024]{3,1,2,0:T(4,128)} %copy-done.10) | copy-start | bytes 98308
  121.8 1.6 copy-start.9
  124.7 64.0 %collective-permute-start = (bf16[4,32,128]{2,1,0:T(8,128)(2,1)S(1)}, bf16[4,32,128]{2,1,0:T(8,128)(2,1)S(1)}, u32[]{:S(2)}, u32[]{:S(2)}) collective-permute-start(bf16[4,32,128]{2,1,0:T(8,128)(2,1)S(1)} %fusion.76), channel_id=1, source_target_pairs={{0,1},{1,0},{2,3},{3,2},{4,5},{5,4},{6,7},{7,6},{8,9},{9,8},{10,11... | collective-permute-start | bytes 98312 | tf_op jit(solution)/shard_map/ppermute | solution.py:21
  132.3 135.6 %all-reduce.7.cloned.1.call-start = ((), (), s32[]{:S(2)}) async-start(), calls=%async_computation.5 | async-start | bytes 131072 | tf_op jit(solution)/shard_map/psum | solution.py:223
  160.8 26.0 %copy-start.7 = (bf16[2048,256,1]{1,0,2:T(8,128)(2,1)S(1)}, bf16[2048,256,1]{1,0,2:T(8,128)(2,1)}, u32[]{:S(2)}) copy-start(bf16[2048,256,1]{1,0,2:T(8,128)(2,1)} %reshape.266) | copy-start | bytes 3145732
  160.8 44.4 %copy-start.13 = (f32[4,128]{1,0:T(4,128)S(1)}, f32[4,128]{1,0:T(4,128)}, u32[]{:S(2)}) copy-start(f32[4,128]{1,0:T(4,128)} %copy-done.12) | copy-start | bytes 6148
  189.3 268.5 %all-reduce.5.cloned.1.call-start = ((), (), s32[]{:S(2)}) async-start(), calls=%async_computation.3 | async-start | bytes 12582912 | tf_op jit(solution)/shard_map/psum | solution.py:220
  212.0 292.1 %reduce-scatter.5.cloned.1.call-start = ((), (), s32[]{:S(2)}) async-start(), calls=%async_computation.2 | async-start | bytes 35651584 | tf_op jit(solution)/shard_map/reduce_scatter | solution.py:200
Sparse Core Ops, SparseCore 0:
  132.4 71.8 reduce-scatter.6
  267.9 208.9 reduce-scatter.4
Sparse Core Ops, SparseCore 1:
  189.4 58.0 all-reduce.6
  252.2 205.6 all-reduce.4
where the time goes:
time: 518 us; the launch traced here: 516 us
  waiting for transfers between devices  203 us (39%)
  matrix products  161 us (31%)
  blocking collectives  66.8 us (13%)
  local copies, waits for them, and re-layouts  38.6 us (7%)
  other arithmetic  29 us (6%)
  between operations  15.7 us (3%)
    psum x1, waiting for transfers between devices, per_device(): down_whole = lax.psum(down_part, ('dp', 'tensor'))  188 us
    dot_general x1, matrix products, per_device(): lax.dot_general(query_gradient_flat, w_query, contract, preferred_element...  55.8 us
    psum x1, blocking collectives, per_device(): lax.psum((square_down, square_q, square_kv), 'tensor')  39.7 us
    all_gather x1, blocking collectives, per_device(): lax.all_gather(low_pick.astype(jnp.bfloat16), 'tensor', axis=1, tiled=True)  27.1 us
    dot_general x1, matrix products, per_device(): lax.dot_general(value_gradient_flat, w_value, contract, preferred_element...  26 us
    dot_general x1, matrix products, per_device(): lax.dot_general(key_gradient_flat, w_key, contract, preferred_element_typ...  25.9 us
    unnamed x5, waiting for transfers between devices  15 us
    dynamic_update_slice x8, local copies, waits for them, and re-layouts, per_device(): lax.map(one_sequence, (q_saved.reshape(sequences, SEQ, local_heads, HD),...  13.5 us
  transfers between devices with their start and end apart: 5, of which 2 were waited for; matrix products, arithmetic and copies ran while one was open for 26% of the time, Pallas kernels for 0%

commit v1 on v0

v1 whole, which is shorter than its diff:
```python
import functools
import math
import numpy as np
import jax
import jax.numpy as jnp
from jax import lax
from jax.experimental import pallas as pl
from jax.experimental.pallas import tpu as pltpu
from jax.sharding import PartitionSpec as P

HD = 128
RANK = 16
TEN = 4
SEQ = 1024
ROPE_BASE = 500000.0
NORM_EPS = 1e-06
MASKED = -1e30
NT = (((1,), (1,)), ((), ()))
TN = (((0,), (0,)), ((), ()))
F32 = jnp.float32
BF16 = jnp.bfloat16
ROWS = 256


def rope_constants():
    half = HD // 2
    freq = ROPE_BASE ** (-(2.0 * np.arange(half)) / HD)
    angle = np.arange(SEQ)[:, None] * freq[None, :]
    cosine = np.concatenate([np.cos(angle), np.cos(angle)], axis=1)
    sine = np.concatenate([np.sin(angle), -np.sin(angle)], axis=1)
    return cosine.astype(np.float32), sine.astype(np.float32)


def attention_kernel(
    ints, q_ref, k_ref, v_ref, g_ref, x_ref, down_ref, upq_ref, upkv_ref, cos_ref, sin_ref,
    grad_ref, dlow_ref, low_ref,
    kt_ref, vt_ref, dk_ref, dv_ref, c_ref, s_ref,
):
    scale = HD ** (-0.5)
    scale2 = scale * math.log2(math.e)
    low_ref[...] = lax.dot_general(
        down_ref[0], x_ref[...], NT, preferred_element_type=F32
    ).astype(BF16)

    def sequence(s, carry):
        base = pl.multiple_of(s * SEQ, SEQ)
        starts = [ints[2 + 4 * s + j] for j in range(4)]
        pos = lax.broadcasted_iota(jnp.int32, (SEQ, HD), 0)
        cb = jnp.broadcast_to(cos_ref[pl.ds(starts[0], 1), :], (SEQ, HD))
        sb = jnp.broadcast_to(sin_ref[pl.ds(starts[0], 1), :], (SEQ, HD))
        for j in range(1, 4):
            inside = pos >= starts[j]
            cb = jnp.where(inside, cos_ref[pl.ds(starts[j], 1), :], cb)
            sb = jnp.where(inside, sin_ref[pl.ds(starts[j], 1), :], sb)
        cp = cos_ref[...]
        sp = sin_ref[...]
        c_ref[...] = cp * cb + sp * sb
        s_ref[...] = sp * cb - cp * sb
        kt_ref[...] = k_ref[pl.ds(base, SEQ), :].T
        vt_ref[...] = v_ref[pl.ds(base, SEQ), :].T
        dk_ref[...] = jnp.zeros_like(dk_ref)
        dv_ref[...] = jnp.zeros_like(dv_ref)
        for h in range(2):
            cols = slice(h * HD, (h + 1) * HD)
            for i in range(SEQ // ROWS):
                width = (i + 1) * ROWS
                rows = pl.ds(base + i * ROWS, ROWS)
                keys = pl.ds(base, width)
                q = q_ref[rows, cols]
                g = g_ref[rows, cols]
                p_row = lax.broadcasted_iota(jnp.int32, (1, ROWS), 1) + i * ROWS
                begin = jnp.zeros((1, ROWS), jnp.int32)
                for j in range(1, 4):
                    begin = jnp.where(p_row >= starts[j], starts[j], begin)
                k_idx = lax.broadcasted_iota(jnp.int32, (width, ROWS), 0)
                allowed = (k_idx >= begin) & (k_idx <= p_row)
                st = lax.dot_general(k_ref[keys, :], q, NT, preferred_element_type=F32)
                st = jnp.where(allowed, st * scale2, MASKED)
                top = jnp.max(st, axis=0, keepdims=True)
                e = jnp.exp2(st - top)
                inv = 1.0 / jnp.sum(e, axis=0, keepdims=True)
                p = e * inv
                p_low = p.astype(BF16)
                ot = jnp.dot(vt_ref[:, :width], p_low, preferred_element_type=F32)
                delta = jnp.sum(g.astype(F32).T * ot, axis=0, keepdims=True)
                dpt = lax.dot_general(v_ref[keys, :], g, NT, preferred_element_type=F32)
                ds_low = (p * (dpt - delta)).astype(BF16)
                dqt = jnp.dot(kt_ref[:, :width], ds_low, preferred_element_type=F32)
                dk_ref[:width, :] += jnp.dot(ds_low, q, preferred_element_type=F32)
                dv_ref[:width, :] += jnp.dot(p_low, g, preferred_element_type=F32)
                dq = dqt.T * scale
                dq = dq * c_ref[i * ROWS : (i + 1) * ROWS, :] + pltpu.roll(
                    dq, HD // 2, 1
                ) * s_ref[i * ROWS : (i + 1) * ROWS, :]
                grad_ref[rows, cols] = dq.astype(BF16)
        dk = dk_ref[...] * scale
        dk = dk * c_ref[...] + pltpu.roll(dk, HD // 2, 1) * s_ref[...]
        grad_ref[pl.ds(base, SEQ), 2 * HD : 3 * HD] = dk.astype(BF16)
        grad_ref[pl.ds(base, SEQ), 3 * HD : 4 * HD] = dv_ref[...].astype(BF16)
        t = ints[s]
        seq_rows = pl.ds(base, SEQ)
        parts = [
            (upq_ref[t], slice(0, 2 * HD)),
            (upkv_ref[t, :RANK, :], slice(2 * HD, 3 * HD)),
            (upkv_ref[t, RANK:, :], slice(3 * HD, 4 * HD)),
        ]
        for n, (up, c) in enumerate(parts):
            back = 2.0 * lax.dot_general(
                up, grad_ref[seq_rows, c], NT, preferred_element_type=F32
            )
            for b in range(8):
                dlow_ref[s * 8 + b, n * RANK : (n + 1) * RANK, :] = back[:, b * 128 : (b + 1) * 128]
        return carry

    lax.fori_loop(0, 2, sequence, 0)


def attention_call(ints, q, k, v, g, x, down, upq, upkv):
    cosine, sine = rope_constants()
    tokens = q.shape[0]
    width = x.shape[1]

    def whole(shape):
        return pl.BlockSpec(shape, lambda i, n: (0,) * len(shape))

    return pl.pallas_call(
        attention_kernel,
        grid_spec=pltpu.PrefetchScalarGridSpec(
            num_scalar_prefetch=1,
            grid=(1,),
            in_specs=[
                whole(q.shape), whole(k.shape), whole(v.shape), whole(g.shape), whole(x.shape),
                pl.BlockSpec((1, 3 * RANK, width), lambda i, n: (n[10], 0, 0)),
                whole(upq.shape), whole(upkv.shape), whole(cosine.shape), whole(sine.shape),
            ],
            out_specs=[whole((tokens, 4 * HD)), whole((16, 48, 128)), whole((48, 128))],
            scratch_shapes=[
                pltpu.VMEM((HD, SEQ), BF16), pltpu.VMEM((HD, SEQ), BF16),
                pltpu.VMEM((SEQ, HD), F32), pltpu.VMEM((SEQ, HD), F32),
                pltpu.VMEM((SEQ, HD), F32), pltpu.VMEM((SEQ, HD), F32),
            ],
        ),
        out_shape=[
            jax.ShapeDtypeStruct((tokens, 4 * HD), BF16),
            jax.ShapeDtypeStruct((16, 48, 128), F32),
            jax.ShapeDtypeStruct((48, 128), BF16),
        ],
        compiler_params=pltpu.CompilerParams(vmem_limit_bytes=56 * 1024 * 1024),
        cost_estimate=pl.CostEstimate(
            flops=6_400_000_000, bytes_accessed=10_000_000, transcendentals=4_000_000
        ),
        name="attention_back",
    )(ints, q, k, v, g, x, down, upq, upkv, cosine, sine)


def from_partner(value, axis, apart):
    mask = 2**apart
    pairs = [(source, source ^ mask) for source in range(lax.axis_size(axis))]
    return lax.ppermute(value, axis, pairs)


def per_device(
    x_rows,
    d_attn,
    q_saved,
    k_saved,
    v_saved,
    w_query,
    w_key,
    w_value,
    down_all,
    up_query,
    up_kv,
    tenant,
    doc_starts,
):
    rows = x_rows.shape[0]
    width = x_rows.shape[1]
    group_tokens = q_saved.shape[0]
    local_heads = q_saved.shape[1] // HD
    sequences = group_tokens // SEQ
    tensor_size = lax.axis_size("tensor")
    here = lax.axis_index("tensor")
    contract = (((1,), (1,)), ((), ()))
    tenant_ids = jnp.arange(TEN, dtype=jnp.int32)
    seq_hot = (tenant[:, None] == tenant_ids[None, :]).astype(jnp.float32)
    token_tenant_onehot = jnp.repeat(seq_hot, SEQ, axis=0)
    row_hot = lax.dynamic_slice_in_dim(token_tenant_onehot, here * rows, rows, 0)
    down_flat = down_all.reshape(TEN * 3 * RANK, width)
    ints = jnp.concatenate(
        [tenant, doc_starts.reshape(-1), lax.dynamic_slice_in_dim(tenant, here // 8, 1)]
    )
    grads, dlow_part, low_own = attention_call(
        ints, q_saved, k_saved, v_saved, d_attn, x_rows, down_all, up_query, up_kv
    )
    low_rows = lax.all_gather(low_own, "tensor", axis=1, tiled=True)
    query_gradient_flat = grads[:, :256]
    key_gradient_flat = grads[:, 256:384]
    value_gradient_flat = grads[:, 384:]
    low_grad = lax.psum_scatter(
        dlow_part.astype(jnp.bfloat16), "tensor", scatter_dimension=0, tiled=True
    )[0].astype(jnp.float32)
    masked_low = low_rows[None, :, :] * token_tenant_onehot.T[:, None, :].astype(jnp.bfloat16)
    query_gradient = 2.0 * jnp.dot(
        masked_low[:, :RANK].reshape(TEN * RANK, group_tokens),
        query_gradient_flat,
        preferred_element_type=jnp.float32,
    ).reshape(TEN, RANK, -1)
    key_gradient = 2.0 * jnp.dot(
        masked_low[:, RANK : 2 * RANK].reshape(TEN * RANK, group_tokens),
        key_gradient_flat,
        preferred_element_type=jnp.float32,
    ).reshape(TEN, RANK, HD)
    value_gradient = 2.0 * jnp.dot(
        masked_low[:, 2 * RANK :].reshape(TEN * RANK, group_tokens),
        value_gradient_flat,
        preferred_element_type=jnp.float32,
    ).reshape(TEN, RANK, HD)
    grad_kv = jnp.concatenate([key_gradient, value_gradient], axis=1)
    grad_kv = grad_kv + from_partner(grad_kv.astype(jnp.bfloat16), "tensor", 0).astype(
        grad_kv.dtype
    )
    total = lax.dot_general(
        query_gradient_flat, w_query, contract, preferred_element_type=jnp.float32
    )
    total = total + lax.dot_general(
        key_gradient_flat, w_key, contract, preferred_element_type=jnp.float32
    )
    frozen = lax.psum_scatter(
        (
            total
            + lax.dot_general(
                value_gradient_flat, w_value, contract, preferred_element_type=jnp.float32
            )
        ).astype(jnp.bfloat16),
        "tensor",
        scatter_dimension=0,
        tiled=True,
    ).astype(jnp.float32)
    spread = (row_hot[:, :, None] * low_grad.T[:, None, :]).reshape(rows, TEN * 3 * RANK)
    down_wide = down_flat.astype(jnp.float32)
    lowrank_dx = jnp.dot(spread, down_wide, precision=lax.Precision.HIGHEST)
    d_rows = (frozen + lowrank_dx).astype(jnp.bfloat16)
    weighted = (row_hot.T[:, None, :] * low_grad[None, :, :]).reshape(TEN * 3 * RANK, rows)
    down_part = jnp.dot(
        weighted, x_rows.astype(jnp.float32), precision=lax.Precision.HIGHEST
    ).reshape(TEN, 3 * RANK, width)
    local_width = width // tensor_size
    down_grad = lax.psum(
        lax.psum_scatter(
            down_part.astype(jnp.bfloat16), "tensor", scatter_dimension=2, tiled=True
        ).astype(jnp.float32),
        "dp",
    )
    query_gradient, grad_kv = (
        lax.psum(query_gradient.astype(jnp.bfloat16), "dp").astype(jnp.float32),
        lax.psum(grad_kv.astype(jnp.bfloat16), "dp").astype(jnp.float32),
    )
    square_down = jnp.sum((down_grad * down_grad).reshape(TEN, 3, -1), axis=2)
    square_q = jnp.sum((query_gradient * query_gradient).reshape(TEN, -1), axis=1)
    square_kv = jnp.sum((grad_kv * grad_kv).reshape(TEN, 2, -1), axis=2)
    total_down, total_q, total_kv = lax.psum((square_down, square_q, square_kv), "tensor")
    count_down = RANK * width
    count_q = RANK * query_gradient.shape[2] * tensor_size
    count_kv = RANK * HD * tensor_size
    upd_down = (
        down_grad.reshape(TEN, 3, RANK, -1)
        / jnp.sqrt(total_down / count_down + NORM_EPS)[:, :, None, None]
    ).reshape(down_grad.shape)
    upd_query = query_gradient / jnp.sqrt(total_q / count_q + NORM_EPS)[:, None, None]
    upd_kv = (
        grad_kv.reshape(TEN, 2, RANK, -1)
        / jnp.sqrt(total_kv / count_kv + NORM_EPS)[:, :, None, None]
    ).reshape(grad_kv.shape)
    return (d_rows, upd_down, upd_query, upd_kv)


def solution(mesh):
    in_specs = (
        P(("dp", "tensor"), None),
        P("dp", "tensor"),
        P("dp", "tensor"),
        P("dp", "tensor"),
        P("dp", "tensor"),
        P(None, "tensor"),
        P(None, "tensor"),
        P(None, "tensor"),
        P(),
        P(None, None, "tensor"),
        P(None, None, "tensor"),
        P("dp"),
        P("dp", None),
    )
    out_specs = (
        P(("dp", "tensor"), None),
        P(None, None, "tensor"),
        P(None, None, "tensor"),
        P(None, None, "tensor"),
    )
    return jax.shard_map(
        per_device, mesh=mesh, in_specs=in_specs, out_specs=out_specs, check_vma=False
    )
```

time: 518 us -> 415 us (0.80)
  waiting for transfers between devices: 203 us -> 142 us
  matrix products: 161 us -> 120 us
  local copies, waits for them, and re-layouts: 38.6 us -> 2.73 us
  blocking collectives: 66.8 us -> 95.2 us
  Pallas kernels: 0 us -> 24.3 us
  other arithmetic: 29 us -> 11.6 us
    psum x1 -> x0, waiting for transfers between devices: 188 us -> none  [per_device(): down_whole = lax.psum(down_part, ('dp', 'tensor'))]
    reduce_scatter x1, waiting for transfers between devices: 0.01 us -> 125 us  [per_device(): lax.psum_scatter((total + lax.dot_general(value_gradient_flat, w_value, c...]
    dot_general x19 -> x3, matrix products: 42.1 us -> 2.41 us  [the longest x1 1.27 us: per_device(): jnp.dot(masked_low[:, 2 * RANK:].reshape(TEN * RANK, group_tokens), value...]
    psum x0 -> x1, blocking collectives: none -> 29.4 us  [per_device(): lax.psum(lax.psum_scatter(down_part.astype(jnp.bfloat16), 'tensor', scatt...]
    pallas_call x0 -> x1, Pallas kernels: none -> 24.3 us  [attention_call(): pl.pallas_call(attention_kernel, grid_spec=pltpu.PrefetchScalarGridSpec(n...]
    reduce_scatter x0 -> x1, waiting for transfers between devices: none -> 17.2 us  [per_device(): lax.psum_scatter(down_part.astype(jnp.bfloat16), 'tensor', scatter_dimens...]
    unnamed x5, waiting for transfers between devices: 15 us -> 0.08 us
    dynamic_update_slice x8 -> x0, local copies, waits for them, and re-layouts: 13.5 us -> none  [per_device(): lax.map(one_sequence, (q_saved.reshape(sequences, SEQ, local_heads, HD),...]
  transfers between devices with their start and end apart: 5 -> 5, of which waited for: 2 -> 2; matrix products, arithmetic and copies ran while one was open for 26% -> 30% of each run, Pallas kernels for 0% -> 0%
where the time goes in v1:
time: 415 us; the launch traced here: 413 us
  waiting for transfers between devices  142 us (34%)
  matrix products  120 us (29%)
  blocking collectives  95.2 us (23%)
  Pallas kernels  24.3 us (6%)
  between operations  15.3 us (4%)
  other arithmetic  11.6 us (3%)
    reduce_scatter x1, waiting for transfers between devices, per_device(): lax.psum_scatter((total + lax.dot_general(value_gradient_flat, w_value, c...  125 us
    dot_general x1, matrix products, per_device(): lax.dot_general(query_gradient_flat, w_query, contract, preferred_element...  56.1 us
    psum x1, blocking collectives, per_device(): lax.psum((square_down, square_q, square_kv), 'tensor')  40.5 us
    psum x1, blocking collectives, per_device(): lax.psum(lax.psum_scatter(down_part.astype(jnp.bfloat16), 'tensor', scatt...  29.4 us
    dot_general x1, matrix products, per_device(): lax.dot_general(key_gradient_flat, w_key, contract, preferred_element_typ...  25.6 us
    all_gather x1, blocking collectives, per_device(): low_rows = lax.all_gather(low_own, 'tensor', axis=1, tiled=True)  25.3 us
    pallas_call x1, Pallas kernels, attention_call(): pl.pallas_call(attention_kernel, grid_spec=pltpu.PrefetchScalarGridSpec(n...  24.3 us
    dot_general x1, matrix products, per_device(): lax.dot_general(value_gradient_flat, w_value, contract, preferred_element...  24.1 us
  transfers between devices with their start and end apart: 5, of which 2 were waited for; matrix products, arithmetic and copies ran while one was open for 30% of the time, Pallas kernels for 0%

profile of v1, /device:TPU:0, one launch (start us, length us, event | category | flops | bytes accessed | tf_op | source)
XLA Modules:
  0.0 413.1 jit_solution(7603607540573205771)
XLA Ops:
  8.1 0.9 reshape.56
  9.0 1.2 dynamic_slice.6
  10.2 1.9 pad_add_fusion.ints
  12.1 24.3 %attention_back.1 = (bf16[2048,512]{1,0:T(8,128)(2,1)}, f32[16,48,128]{2,1,0:T(8,128)}, bf16[48,128]{1,0:T(8,128)(2,1)}) custom-call(s32[11]{0:T(128)} %pad_add_fusion.ints, bf16[2048,256]{1,0:T(8,128)(2,1)} %q_ref.1, bf16[2048,128]{1,0:T(8,128)(2,1)} %k_ref.1, bf16[2048,128]{1,0:T(8,128)(2,1)} %v_ref.1, bf16[2048,256]{1,0:T(8,128)(2,1)} %g_ref.1, ...), custom_call_target="tpu_custom_call" | custom-call | flops 6400000000 | bytes 10000000 | tf_op jit(solution)/shard_map/attention_back/pallas_call | solution.py:126
  36.4 1.7 convert_element_type.56
  38.3 25.3 %all_gather.3 = bf16[48,2048]{1,0:T(8,128)(2,1)S(1)} all-gather(bf16[48,128]{1,0:T(8,128)(2,1)} %get-tuple-element.9), channel_id=1, replica_groups=mesh['dp'=8,'tensor'=16] {'tensor'}, dimensions={1}, use_global_device_ids=true | all-gather | bytes 208896 | tf_op jit(solution)/shard_map/all_gather | solution.py:196
  63.7 1.3 convolution_multiply_fusion.1
  65.0 0.2 convolution_multiply_fusion.2
  65.2 1.5 collective-permute-start
  66.7 24.1 %fusion.10 = f32[2048,8192]{1,0:T(8,128)} fusion(bf16[8192,128]{1,0:T(8,128)(2,1)S(1)} %copy-done, bf16[2048,512]{1,0:T(8,128)(2,1)S(1)} %copy-done.1), kind=kOutput, calls=%fused_computation.16 | convolution fusion | flops 4294967296 | bytes 69730304 | tf_op jit(solution)/shard_map/dot_general | solution.py:232
  90.9 25.6 %fusion.13 = f32[2048,8192]{1,0:T(8,128)} fusion(bf16[8192,128]{1,0:T(8,128)(2,1)} %param.21, bf16[2048,512]{1,0:T(8,128)(2,1)S(1)} %copy-done.1), kind=kOutput, calls=%fused_computation.19 | convolution fusion | flops 4294967296 | bytes 69730304 | tf_op jit(solution)/shard_map/dot_general | solution.py:226
  116.5 0.9 fusion.3
  117.4 1.4 add_convert_fusion.1
  118.9 0.7 bitcast_convert_fusion
  119.6 5.8 %convolution_convert_fusion = bf16[4,48,8192]{2,1,0:T(8,128)(2,1)} fusion(bf16[128,8192]{1,0:T(8,128)(2,1)} %x_ref.1, f32[48,128]{1,0:T(8,128)S(1)} %get-tuple-element.15, f32[4,128]{1,0:T(4,128)S(1)} %fusion.33), kind=kOutput, calls=%fused_computation.1 | convolution fusion | flops 2417516544 | bytes 5269504 | tf_op jit(solution)/shard_map/dot_general | solution.py:245
  125.5 56.1 %add_convert_fusion = bf16[2048,8192]{1,0:T(8,128)(2,1)} fusion(f32[2048,8192]{1,0:T(8,128)} %fusion.10, f32[2048,8192]{1,0:T(8,128)} %fusion.13, bf16[8192,256]{1,0:T(8,128)(2,1)} %param.20, bf16[2048,512]{1,0:T(8,128)(2,1)} %get-tuple-element.7), kind=kOutput, calls=%fused_computation | convolution fusion | flops 8640266240 | bytes 173015040 | tf_op jit(solution)/shard_map/dot_general | solution.py:223
  181.7 0.8 fusion.21
  182.6 0.1 reduce_sum.47
  182.7 0.9 fusion.20
  183.6 17.2 %reduce-scatter.8.cloned.1.call-done = bf16[4,48,512]{2,1,0:T(8,128)(2,1)} async-done(((bf16[4,48,8192]{2,1,0:T(8,128)(2,1)}), bf16[4,48,512]{2,1,0:T(8,128)(2,1)}) %reduce-scatter.8.cloned.1.call-update) | async-done | bytes 196624 | tf_op jit(solution)/shard_map/reduce_scatter | solution.py:250
  200.8 29.4 %all-reduce.7 = f32[4,48,512]{2,1,0:T(8,128)S(1)} all-reduce(bf16[4,48,512]{2,1,0:T(8,128)(2,1)} %reduce-scatter.8.cloned.1.call-done), channel_id=1, replica_groups=mesh['dp'=8,'tensor'=16] {'dp'}, use_global_device_ids=true, to_apply=%region_3.4 | all-reduce | flops 98304 | bytes 589824 | tf_op jit(solution)/shard_map/psum | solution.py:249
  230.1 0.1 multiply_reduce_fusion
  230.2 0.1 reduce_sum.32
  230.3 0.1 reduce_sum.36
  230.4 40.5 %all-reduce.1 = (f32[4,3]{1,0:T(4,128)S(1)}, f32[4]{0:T(128)S(1)}, f32[4,2]{1,0:T(4,128)S(1)}) all-reduce(f32[4,3]{1,0:T(4,128)S(1)} %reduce_sum.36, f32[4]{0:T(128)S(1)} %fusion.20, f32[4,2]{1,0:T(4,128)S(1)} %reduce_sum.47), channel_id=1, replica_groups=mesh['dp'=8,'tensor'=16] {'tensor'}, use_global_device_ids=true, to_apply=%region_6.7 | all-reduce | flops 24 | bytes 192 | tf_op jit(solution)/shard_map/psum | solution.py:262
  271.0 0.1 div.64
  271.2 0.1 div.56
  271.3 1.5 convert_divide_fusion.1
  272.8 1.5 convert_divide_fusion
  274.2 0.8 broadcast_divide_fusion
  275.1 125.1 %reduce-scatter.6.cloned.1.call-done = bf16[128,8192]{1,0:T(8,128)(2,1)} async-done(((bf16[2048,8192]{1,0:T(8,128)(2,1)}), bf16[128,8192]{1,0:T(8,128)(2,1)}) %reduce-scatter.6.cloned.1.call-update) | async-done | bytes 2097168 | tf_op jit(solution)/shard_map/reduce_scatter | solution.py:229
  400.1 5.9 %fusion.1 = bf16[128,8192]{1,0:T(8,128)(2,1)} fusion(bf16[4,48,8192]{2,1,0:T(8,128)(2,1)} %down_ref.1, bf16[128,8192]{1,0:T(8,128)(2,1)} %reduce-scatter.6.cloned.1.call-done, f32[128,48]{0,1:T(8,128)S(1)} %get-tuple-element.16, f32[128,4]{0,1:T(4,128)S(1)} %constant_dynamic-slice_fusion), kind=kOutput, calls=%fused_computation.4 | convolution fusion | flops 2419089408 | bytes 7366656 | tf_op jit(solution)/shard_map/dot_general | solution.py:242
  (31 shorter events, 0.7 us)
Async XLA Ops:
  8.0 58.7 %copy-start = (bf16[8192,128]{1,0:T(8,128)(2,1)S(1)}, bf16[8192,128]{1,0:T(8,128)(2,1)}, u32[]{:S(2)}) copy-start(bf16[8192,128]{1,0:T(8,128)(2,1)} %param.22) | copy-start | bytes 6291460
  8.0 110.9 %reduce-scatter.10.cloned.1.call-start = ((), (), s32[]{:S(2)}) async-start(), calls=%async_computation.5 | async-start | bytes 208896
  12.1 26.1 %copy-start.2 = (s32[2]{0:T(128)S(1)}, s32[2]{0:T(128)}, u32[]{:S(2)}) copy-start(s32[2]{0:T(128)} %param.26) | copy-start | bytes 28
  38.1 143.6 %all-reduce.6.cloned.1.call-start = ((), (), s32[]{:S(2)}) async-start(), calls=%async_computation.6 | async-start | bytes 131072 | tf_op jit(solution)/shard_map/psum | solution.py:256
  38.2 26.8 %copy-start.1 = (bf16[2048,512]{1,0:T(8,128)(2,1)S(1)}, bf16[2048,512]{1,0:T(8,128)(2,1)}, u32[]{:S(2)}) copy-start(bf16[2048,512]{1,0:T(8,128)(2,1)} %get-tuple-element.7) | copy-start | bytes 6291460
  65.2 52.2 %collective-permute-start = (bf16[4,32,128]{2,1,0:T(8,128)(2,1)S(1)}, bf16[4,32,128]{2,1,0:T(8,128)(2,1)}, u32[]{:S(2)}, u32[]{:S(2)}) collective-permute-start(bf16[4,32,128]{2,1,0:T(8,128)(2,1)S(1)} %fusion.22), channel_id=1, source_target_pairs={{0,1},{1,0},{2,3},{3,2},{4,5},{5,4},{6,7},{7,6},{8,9},{9,8},{10,11... | collective-permute-start | bytes 98312 | tf_op jit(solution)/shard_map/ppermute | solution.py:159
  118.8 81.9 %reduce-scatter.8.cloned.1.call-start = ((), (), s32[]{:S(2)}) async-start(), calls=%async_computation.4 | async-start | bytes 3342336 | tf_op jit(solution)/shard_map/reduce_scatter | solution.py:250
  125.4 274.7 %reduce-scatter.6.cloned.1.call-start = ((), (), s32[]{:S(2)}) async-start(), calls=%async_computation.3 | async-start | bytes 35651584 | tf_op jit(solution)/shard_map/reduce_scatter | solution.py:229
Sparse Core Ops, SparseCore 0:
  38.2 73.8 reduce-scatter.9
  125.6 75.1 reduce-scatter.7
  204.7 195.3 reduce-scatter.5
Sparse Core Ops, SparseCore 1:
  118.9 58.4 all-reduce.5

commit v2 on v1

v2 whole, which is shorter than its diff:
```python
import functools
import math
import numpy as np
import jax
import jax.numpy as jnp
from jax import lax
from jax.experimental import pallas as pl
from jax.experimental.pallas import tpu as pltpu
from jax.sharding import PartitionSpec as P

HD = 128
RANK = 16
TEN = 4
SEQ = 1024
ROPE_BASE = 500000.0
NORM_EPS = 1e-06
MASKED = -1e30
NT = (((1,), (1,)), ((), ()))
TN = (((0,), (0,)), ((), ()))
F32 = jnp.float32
BF16 = jnp.bfloat16
ROWS = 256


def rope_constants():
    half = HD // 2
    freq = ROPE_BASE ** (-(2.0 * np.arange(half)) / HD)
    angle = np.arange(SEQ)[:, None] * freq[None, :]
    cosine = np.concatenate([np.cos(angle), np.cos(angle)], axis=1)
    sine = np.concatenate([np.sin(angle), -np.sin(angle)], axis=1)
    return cosine.astype(np.float32), sine.astype(np.float32)


def attention_kernel(
    tenant_ref, doc_ref, q_ref, k_ref, v_ref, g_ref, x_ref, down_ref, upq_ref, upkv_ref,
    cos_ref, sin_ref,
    grad_ref, dlow_ref, low_ref, hot_ref, dsel_ref,
    kt_ref, vt_ref, dk_ref, dv_ref, c_ref, s_ref, down_sem,
):
    own = tenant_ref[lax.axis_index("tensor") // 8]
    fetch = pltpu.make_async_copy(down_ref.at[own], dsel_ref, down_sem)
    fetch.start()
    for s in range(2):
        for t in range(TEN):
            hot_ref[4 * s + t : 4 * s + t + 1, :] = jnp.where(
                jnp.full((1, 128), tenant_ref[s]) == t, 1.0, 0.0
            )
    scale = HD ** (-0.5)
    scale2 = scale * math.log2(math.e)

    def sequence(s, carry):
        base = pl.multiple_of(s * SEQ, SEQ)
        starts = [doc_ref[s, j] for j in range(4)]
        pos = lax.broadcasted_iota(jnp.int32, (SEQ, HD), 0)
        cb = jnp.broadcast_to(cos_ref[pl.ds(starts[0], 1), :], (SEQ, HD))
        sb = jnp.broadcast_to(sin_ref[pl.ds(starts[0], 1), :], (SEQ, HD))
        for j in range(1, 4):
            inside = pos >= starts[j]
            cb = jnp.where(inside, cos_ref[pl.ds(starts[j], 1), :], cb)
            sb = jnp.where(inside, sin_ref[pl.ds(starts[j], 1), :], sb)
        cp = cos_ref[...]
        sp = sin_ref[...]
        c_ref[...] = cp * cb + sp * sb
        s_ref[...] = sp * cb - cp * sb
        kt_ref[...] = k_ref[pl.ds(base, SEQ), :].T
        vt_ref[...] = v_ref[pl.ds(base, SEQ), :].T
        dk_ref[...] = jnp.zeros_like(dk_ref)
        dv_ref[...] = jnp.zeros_like(dv_ref)
        for h in range(2):
            cols = slice(h * HD, (h + 1) * HD)
            for i in range(SEQ // ROWS):
                width = (i + 1) * ROWS
                rows = pl.ds(base + i * ROWS, ROWS)
                keys = pl.ds(base, width)
                q = q_ref[rows, cols]
                g = g_ref[rows, cols]
                p_row = lax.broadcasted_iota(jnp.int32, (1, ROWS), 1) + i * ROWS
                begin = jnp.zeros((1, ROWS), jnp.int32)
                for j in range(1, 4):
                    begin = jnp.where(p_row >= starts[j], starts[j], begin)
                k_idx = lax.broadcasted_iota(jnp.int32, (width, ROWS), 0)
                allowed = (k_idx >= begin) & (k_idx <= p_row)
                st = lax.dot_general(k_ref[keys, :], q, NT, preferred_element_type=F32)
                st = jnp.where(allowed, st * scale2, MASKED)
                top = jnp.max(st, axis=0, keepdims=True)
                e = jnp.exp2(st - top)
                inv = 1.0 / jnp.sum(e, axis=0, keepdims=True)
                p = e * inv
                p_low = p.astype(BF16)
                ot = jnp.dot(vt_ref[:, :width], p_low, preferred_element_type=F32)
                delta = jnp.sum(g.astype(F32).T * ot, axis=0, keepdims=True)
                dpt = lax.dot_general(v_ref[keys, :], g, NT, preferred_element_type=F32)
                ds_low = (p * (dpt - delta)).astype(BF16)
                dqt = jnp.dot(kt_ref[:, :width], ds_low, preferred_element_type=F32)
                dk_ref[:width, :] += jnp.dot(ds_low, q, preferred_element_type=F32)
                dv_ref[:width, :] += jnp.dot(p_low, g, preferred_element_type=F32)
                dq = dqt.T * scale
                dq = dq * c_ref[i * ROWS : (i + 1) * ROWS, :] + pltpu.roll(
                    dq, HD // 2, 1
                ) * s_ref[i * ROWS : (i + 1) * ROWS, :]
                grad_ref[rows, cols] = dq.astype(BF16)
        dk = dk_ref[...] * scale
        dk = dk * c_ref[...] + pltpu.roll(dk, HD // 2, 1) * s_ref[...]
        grad_ref[pl.ds(base, SEQ), 2 * HD : 3 * HD] = dk.astype(BF16)
        grad_ref[pl.ds(base, SEQ), 3 * HD : 4 * HD] = dv_ref[...].astype(BF16)
        t = tenant_ref[s]
        seq_rows = pl.ds(base, SEQ)
        parts = [
            (upq_ref[t], slice(0, 2 * HD)),
            (upkv_ref[t, :RANK, :], slice(2 * HD, 3 * HD)),
            (upkv_ref[t, RANK:, :], slice(3 * HD, 4 * HD)),
        ]
        for n, (up, c) in enumerate(parts):
            back = 2.0 * lax.dot_general(
                up, grad_ref[seq_rows, c], NT, preferred_element_type=F32
            )
            for b in range(8):
                dlow_ref[s * 8 + b, n * RANK : (n + 1) * RANK, :] = back[:, b * 128 : (b + 1) * 128]
        return carry

    lax.fori_loop(0, 2, sequence, 0)
    fetch.wait()
    low_ref[...] = lax.dot_general(
        dsel_ref[...], x_ref[...], NT, preferred_element_type=F32
    ).astype(BF16)


def attention_call(tenant, docs, q, k, v, g, x, down, upq, upkv):
    cosine, sine = rope_constants()
    tokens = q.shape[0]
    vmem = pl.BlockSpec(memory_space=pltpu.VMEM)
    smem = pl.BlockSpec(memory_space=pltpu.SMEM)
    return pl.pallas_call(
        attention_kernel,
        in_specs=[smem] * 2 + [vmem] * 5 + [pl.BlockSpec(memory_space=pl.ANY)] + [vmem] * 4,
        out_specs=[vmem] * 5,
        scratch_shapes=[
            pltpu.VMEM((HD, SEQ), BF16), pltpu.VMEM((HD, SEQ), BF16),
            pltpu.VMEM((SEQ, HD), F32), pltpu.VMEM((SEQ, HD), F32),
            pltpu.VMEM((SEQ, HD), F32), pltpu.VMEM((SEQ, HD), F32),
            pltpu.SemaphoreType.DMA,
        ],
        out_shape=[
            jax.ShapeDtypeStruct((tokens, 4 * HD), BF16),
            jax.ShapeDtypeStruct((16, 48, 128), F32),
            jax.ShapeDtypeStruct((48, 128), BF16),
            jax.ShapeDtypeStruct((8, 128), F32),
            jax.ShapeDtypeStruct((48, x.shape[1]), BF16),
        ],
        compiler_params=pltpu.CompilerParams(vmem_limit_bytes=56 * 1024 * 1024),
        cost_estimate=pl.CostEstimate(
            flops=6_400_000_000, bytes_accessed=10_000_000, transcendentals=4_000_000
        ),
        name="attention_back",
    )(tenant, docs, q, k, v, g, x, down, upq, upkv, cosine, sine)


MESH_ID = pl.DeviceIdType.MESH
CHUNK = 256
QUARTER = 512
BLOCK_D = 2048
ORDER = ((2, 0), (2, 1), (1, 0), (3, 1), (1, 1), (3, 0), (0, 1), (0, 0))


def exchange_kernel(
    grad_ref, dlow_ref, low_ref, hot_ref, x_ref, dsel_ref,
    wq_ref, wk_ref, wv_ref, p1_ref, p2_ref, p3_ref, c1_ref, c2_ref, c3_ref,
    out_ref, ud_ref, uq_ref, ukv_ref,
    gall, a_ref, wx, part, zbuf, fbuf, fin,
    dlall, lowall, lowcat, dlw_ref, kvown, kvpeer, qown, gdown, gdall, dsum,
    rsbuf, rsall, agbuf, sqall,
    wsem, gsend, grecv, dlsend, dlrecv, lowsend, lowrecv, kvsem, dnsend, dnrecv,
    rssend, rsrecv, agsend, agrecv, sqsend, sqrecv, zsend, zrecv, fsend, frecv,
):
    me_dp = lax.axis_index("dp")
    me_t = lax.axis_index("tensor")
    z = me_t // 4
    x = me_t % 4
    core = me_dp % 2
    xr, xl, xo = (x + 1) % 4, (x + 3) % 4, (x + 2) % 4
    pair = x + 1 - 2 * (x % 2)
    mirror = 3 - x
    z_right = ((z + 1) % 4) * 4 + x
    z_left = ((z + 3) % 4) * 4 + x

    def remote(src, dst, ssem, rsem, dp, t):
        return pltpu.make_async_remote_copy(
            src_ref=src, dst_ref=dst, send_sem=ssem, recv_sem=rsem,
            device_id=(dp, t), device_id_type=MESH_ID,
        )

    barrier = pltpu.get_barrier_semaphore()

    def greet_tensor(o, c):
        pl.semaphore_signal(
            barrier, inc=1, device_id=(me_dp, (me_t + o) % 16), device_id_type=MESH_ID
        )
        return c

    def greet_dp(o, c):
        pl.semaphore_signal(
            barrier, inc=1, device_id=((me_dp + o) % 8, me_t), device_id_type=MESH_ID
        )
        return c

    lax.fori_loop(1, 16, greet_tensor, 0)
    lax.fori_loop(1, 8, greet_dp, 0)

    mine = pl.multiple_of(core * 1024, 1024)
    other = pl.multiple_of((1 - core) * 1024, 1024)
    d0 = pl.multiple_of(x * BLOCK_D, BLOCK_D)
    kv_here = 4 + x // 2
    kv_there = 5 - x // 2

    def piece(i, src, dst):
        return pltpu.make_async_copy(src, dst, wsem.at[i])

    w_copies = [
        piece(0, wq_ref.at[pl.ds(d0, BLOCK_D), :], wx.at[x]),
        piece(1, wk_ref.at[pl.ds(d0, BLOCK_D), :], wx.at[kv_here, :, pl.ds(0, 128)]),
        piece(2, wv_ref.at[pl.ds(d0, BLOCK_D), :], wx.at[kv_here, :, pl.ds(128, 128)]),
    ]
    for n, (row, refs) in enumerate(((mine, (p1_ref, p2_ref, p3_ref)), (other, (c1_ref, c2_ref, c3_ref)))):
        i = 3 + 5 * n
        w_copies += [
            piece(i, refs[0], wx.at[pair, pl.ds(row, 1024), :]),
            piece(i + 1, refs[1].at[pl.ds(0, 1024), :], wx.at[xo, pl.ds(row, 1024), :]),
            piece(i + 2, refs[1].at[pl.ds(1024, 512), :], wx.at[kv_there, pl.ds(row, 512), :]),
            piece(i + 3, refs[2].at[pl.ds(0, 1024), :], wx.at[mirror, pl.ds(row, 1024), :]),
            piece(
                i + 4, refs[2].at[pl.ds(1024, 512), :],
                wx.at[kv_there, pl.ds(pl.multiple_of(row + 512, 512), 512), :],
            ),
        ]
    for copy in w_copies:
        copy.start()

    pl.semaphore_wait(barrier, 22)

    def first_row(c):
        off, half = ORDER[c]
        return pl.multiple_of(((z + off) % 4) * QUARTER + half * CHUNK, CHUNK)

    def gather_out(c):
        rows = pl.ds(first_row(c), CHUNK)
        src = grad_ref.at[rows, :]
        dst = gall.at[x, rows, :]
        return (
            remote(src, dst, gsend.at[0, c], grecv.at[0, c], me_dp, z * 4 + xr),
            remote(src, dst, gsend.at[1, c], grecv.at[1, c], me_dp, z * 4 + xl),
        )

    def gather_in(c):
        rows = pl.ds(first_row(c), CHUNK)
        from_l = gall.at[xl, rows, :]
        from_r = gall.at[xr, rows, :]
        return (
            remote(from_l, from_l, gsend.at[0, c], grecv.at[0, c], me_dp, z * 4 + xr),
            remote(from_r, from_r, gsend.at[1, c], grecv.at[1, c], me_dp, z * 4 + xl),
        )

    def forward_out(c):
        r0 = first_row(c)
        to_r = gall.at[xl, pl.ds(r0, CHUNK // 2), :]
        to_l = gall.at[xr, pl.ds(pl.multiple_of(r0 + CHUNK // 2, CHUNK // 2), CHUNK // 2), :]
        return (
            remote(to_r, to_r, gsend.at[2, c], grecv.at[2, c], me_dp, z * 4 + xr),
            remote(to_l, to_l, gsend.at[3, c], grecv.at[3, c], me_dp, z * 4 + xl),
        )

    def forward_in(c):
        r0 = first_row(c)
        from_l = gall.at[xo, pl.ds(r0, CHUNK // 2), :]
        from_r = gall.at[xo, pl.ds(pl.multiple_of(r0 + CHUNK // 2, CHUNK // 2), CHUNK // 2), :]
        return (
            remote(from_l, from_l, gsend.at[2, c], grecv.at[2, c], me_dp, z * 4 + xr),
            remote(from_r, from_r, gsend.at[3, c], grecv.at[3, c], me_dp, z * 4 + xl),
        )

    def start(copies):
        for copy in copies:
            copy.start()

    def arrive(c):
        for copy in gather_in(c):
            copy.wait_recv()
        start(forward_out(c))

    def to_tensor(src, buf, ssem, rsem, picked):
        def descriptor(t):
            return remote(
                src.at[t] if picked else src, buf.at[me_t], ssem.at[t], rsem.at[me_t], me_dp, t
            )

        def begin(o, c):
            descriptor((me_t + o) % 16).start()
            return c

        def receive(o, c):
            t = (me_t + o) % 16
            remote(buf.at[t], buf.at[t], ssem.at[t], rsem.at[t], me_dp, t).wait_recv()
            return c

        def sent(o, c):
            descriptor((me_t + o) % 16).wait_send()
            return c

        return (
            lambda: lax.fori_loop(1, 16, begin, 0),
            lambda: lax.fori_loop(1, 16, receive, 0),
            lambda: lax.fori_loop(1, 16, sent, 0),
        )

    def to_dp(src_at, buf, ssem, rsem):
        def descriptor(d):
            return remote(src_at(d), buf.at[me_dp], ssem.at[d], rsem.at[me_dp], d, me_t)

        def begin(o, c):
            descriptor((me_dp + o) % 8).start()
            return c

        def receive(o, c):
            d = (me_dp + o) % 8
            remote(buf.at[d], buf.at[d], ssem.at[d], rsem.at[d], d, me_t).wait_recv()
            return c

        def sent(o, c):
            descriptor((me_dp + o) % 8).wait_send()
            return c

        return (
            lambda: lax.fori_loop(1, 8, begin, 0),
            lambda: lax.fori_loop(1, 8, receive, 0),
            lambda: lax.fori_loop(1, 8, sent, 0),
        )

    dl_start, dl_recv, dl_sent = to_tensor(dlow_ref, dlall, dlsend, dlrecv, True)
    low_start, low_recv, low_sent = to_tensor(low_ref, lowall, lowsend, lowrecv, False)
    dn_start, dn_recv, dn_sent = to_tensor(gdown, gdall, dnsend, dnrecv, True)
    sq_start, sq_recv, sq_sent = to_tensor(sqall.at[me_t], sqall, sqsend, sqrecv, False)
    rs_start, rs_recv, rs_sent = to_dp(lambda d: rsbuf.at[d], rsall, rssend, rsrecv)
    ag_start, ag_recv, ag_sent = to_dp(lambda d: agbuf.at[me_dp], agbuf, agsend, agrecv)
    kv_copy = remote(kvown, kvpeer, kvsem.at[0], kvsem.at[1], me_dp, z * 4 + pair)

    start(gather_out(0))
    dl_start()
    low_start()
    start(gather_out(1))
    start(gather_out(2))
    dlall[me_t] = dlow_ref[me_t]
    lowall[me_t] = low_ref[...]
    gall[x] = grad_ref[...]

    def step_low():
        low_recv()
        for b in range(16):
            lowcat[:, b * 128 : (b + 1) * 128] = lowall[b]
        for s in range(2):
            rows = slice(s * SEQ, (s + 1) * SEQ)
            qown[s] = 2.0 * jnp.dot(
                lowcat[:RANK, rows], grad_ref[rows, 0:256], preferred_element_type=F32
            )
            kvown[s, :RANK, :] = 2.0 * jnp.dot(
                lowcat[RANK : 2 * RANK, rows], grad_ref[rows, 256:384], preferred_element_type=F32
            )
            kvown[s, RANK:, :] = 2.0 * jnp.dot(
                lowcat[2 * RANK :, rows], grad_ref[rows, 384:512], preferred_element_type=F32
            )
        kv_copy.start()

    def step_dlow():
        dl_recv()
        total = dlall[0]
        for b in range(1, 16):
            total = total + dlall[b]
        dlw_ref[...] = total.astype(BF16)

        def column(t, c):
            gdown[t] = jnp.dot(
                dlw_ref[...], x_ref[:, pl.ds(pl.multiple_of(t * 512, 512), 512)],
                preferred_element_type=F32,
            ).astype(BF16)
            return c

        lax.fori_loop(0, 16, column, 0)
        dn_start()
        gdall[me_t] = gdown[me_t]

    def step_down():
        dn_recv()
        kv_copy.wait_recv()
        for s in range(2):
            total = gdall[8 * s].astype(F32)
            for b in range(1, 8):
                total = total + gdall[8 * s + b].astype(F32)
            dsum[s] = total
            kvown_sum = kvown[s] + kvpeer[s]
            kvpeer[s] = kvown_sum
        for j in range(8):
            cb = j % 4
            for i in range(2):
                t = 2 * (j // 4) + i
                rsbuf[j, 48 * i : 48 * (i + 1), :] = (
                    dsum[0, :, cb * 128 : (cb + 1) * 128] * hot_ref[t : t + 1, :]
                    + dsum[1, :, cb * 128 : (cb + 1) * 128] * hot_ref[4 + t : 5 + t, :]
                )
            t = j // 2
            c = j % 2
            rsbuf[j, 96:112, :] = (
                qown[0, :, c * 128 : (c + 1) * 128] * hot_ref[t : t + 1, :]
                + qown[1, :, c * 128 : (c + 1) * 128] * hot_ref[4 + t : 5 + t, :]
            )
            rsbuf[j, 112:128, :] = (
                kvpeer[0, c * 16 : (c + 1) * 16, :] * hot_ref[t : t + 1, :]
                + kvpeer[1, c * 16 : (c + 1) * 16, :] * hot_ref[4 + t : 5 + t, :]
            )
        rs_start()
        rsall[me_dp] = rsbuf[me_dp]

    def step_reduce():
        rs_recv()
        total = rsall[0]
        for b in range(1, 8):
            total = total + rsall[b]
        agbuf[me_dp] = total
        ag_start()

    def parts_of(t):
        for n in range(3):
            lo = (t % 2) * 48 + n * 16
            yield [(t // 2) * 4 + cb for cb in range(4)], slice(lo, lo + 16)
        yield [2 * t, 2 * t + 1], slice(96, 112)
        yield [2 * t], slice(112, 128)
        yield [2 * t + 1], slice(112, 128)

    def step_squares():
        ag_recv()
        row = lax.broadcasted_iota(jnp.int32, (8, 128), 0)
        lane = lax.broadcasted_iota(jnp.int32, (8, 128), 1)
        tile = jnp.zeros((8, 128), F32)
        for t in range(TEN):
            for n, (pieces, rows) in enumerate(parts_of(t)):
                total = None
                for j in pieces:
                    v = agbuf[j, rows, :]
                    total = v * v if total is None else total + v * v
                value = jnp.sum(
                    jnp.sum(total, axis=0, keepdims=True), axis=1, keepdims=True
                )
                tile = jnp.where((row == t) & (lane == n), value, tile)
        sqall[me_t] = tile
        sq_start()

    def step_update():
        sq_recv()
        total = sqall[0]
        for b in range(1, 16):
            total = total + sqall[b]
        for t in range(TEN):
            for n, (pieces, rows) in enumerate(parts_of(t)):
                count = RANK * (8192 if n < 3 else 4096 if n == 3 else 2048)
                factor = 1.0 / jnp.sqrt(total[t : t + 1, n : n + 1] * (1.0 / count) + NORM_EPS)
                for i, j in enumerate(pieces):
                    value = agbuf[j, rows, :] * factor
                    if n < 3:
                        ud_ref[t, n * 16 : (n + 1) * 16, i * 128 : (i + 1) * 128] = value
                    elif n == 3:
                        uq_ref[t, :, i * 128 : (i + 1) * 128] = value
                    else:
                        ukv_ref[t, (n - 4) * 16 : (n - 3) * 16, :] = value

    def product(c, write, added):
        rows = pl.ds(first_row(c), CHUNK)
        for b in range(4):
            a_ref[b] = gall[b, rows, 0:256]
        for b in range(2):
            a_ref[4 + b] = (
                gall[2 * b, rows, 256:512].astype(F32) + gall[2 * b + 1, rows, 256:512].astype(F32)
            ).astype(BF16)

        def tile(n, carry):
            cols = pl.ds(pl.multiple_of(n * 512, 512), 512)
            acc = lax.dot_general(a_ref[0], wx[0, cols, :], NT, preferred_element_type=F32)
            for b in range(1, 6):
                acc = acc + lax.dot_general(
                    a_ref[b], wx[b, cols, :], NT, preferred_element_type=F32
                )
            for ref in added:
                acc = acc + ref[:, cols].astype(F32)
            write(cols, acc)
            return carry

        lax.fori_loop(0, 4, tile, 0)

    def z_copy(i):
        to = z_right if i % 2 == 0 else z_left
        return remote(part.at[i], zbuf.at[i], zsend.at[i], zrecv.at[i], me_dp, to)

    def to_part(i):
        def write(cols, acc):
            part[i, :, cols] = acc.astype(BF16)

        return write

    def to_final(half):
        def write(cols, acc):
            fbuf[2 * half, :, cols] = acc[:128].astype(BF16)
            fbuf[2 * half + 1, :, cols] = acc[128:].astype(BF16)

        return write

    def final_copy(o):
        return remote(fbuf.at[o], fin.at[x], fsend.at[o], frecv.at[x], me_dp, z * 4 + o)

    steps = (step_dlow, step_low, step_down, step_reduce, step_squares, step_update)
    arrive(0)
    for copy in w_copies:
        copy.wait()
    for c in range(8):
        if c + 1 < 8:
            arrive(c + 1)
        if c + 3 < 8:
            start(gather_out(c + 3))
        for copy in forward_in(c):
            copy.wait_recv()
        if c < 6:
            added = []
            if c in (2, 3):
                z_copy(c - 2).wait_recv()
                added = [zbuf.at[c - 2]]
            product(c, to_part(c), added)
            z_copy(c).start()
            steps[c]()
        else:
            half = ORDER[c][1]
            sources = (4, 3) if half == 1 else (2, 5)
            for i in sources:
                z_copy(i).wait_recv()
            product(c, to_final(half), [zbuf.at[i] for i in sources])
            for o in (2 * half, 2 * half + 1):

                @pl.when(x != o)
                def _(o=o):
                    final_copy(o).start()

    fin[x] = fbuf[x]
    for o in range(1, 4):
        xs = (x + o) % 4
        remote(fin.at[xs], fin.at[xs], fsend.at[xs], frecv.at[xs], me_dp, z * 4 + xs).wait_recv()
    for b in range(4):
        for n in range(4):
            cols = slice(b * BLOCK_D + n * 512, b * BLOCK_D + (n + 1) * 512)
            low_rank = lax.dot_general(
                dlw_ref[...], dsel_ref[:, cols], TN, preferred_element_type=F32
            )
            out_ref[:, cols] = (
                fin[b, :, n * 512 : (n + 1) * 512].astype(F32) + low_rank
            ).astype(BF16)

    for c in range(8):
        for copy in gather_out(c) + forward_out(c):
            copy.wait_send()
    for sent in (dl_sent, low_sent, dn_sent, sq_sent, rs_sent, ag_sent):
        sent()
    kv_copy.wait_send()
    for i in range(6):
        z_copy(i).wait_send()
    for o in range(4):

        @pl.when(x != o)
        def _(o=o):
            final_copy(o).wait_send()


def exchange_call(grad, dlow, low, hot, x, dsel, wq, wk, wv, pieces):
    vmem = pl.BlockSpec(memory_space=pltpu.VMEM)
    hbm = pl.BlockSpec(memory_space=pl.ANY)
    dma = pltpu.SemaphoreType.DMA
    tokens = grad.shape[0]
    return pl.pallas_call(
        exchange_kernel,
        in_specs=[vmem] * 6 + [hbm] * 9,
        out_specs=[vmem] * 4,
        out_shape=[
            jax.ShapeDtypeStruct(x.shape, BF16),
            jax.ShapeDtypeStruct((TEN, 48, 512), F32),
            jax.ShapeDtypeStruct((TEN, RANK, 256), F32),
            jax.ShapeDtypeStruct((TEN, 2 * RANK, 128), F32),
        ],
        scratch_shapes=[
            pltpu.VMEM((4, tokens, 512), BF16),
            pltpu.VMEM((6, CHUNK, 256), BF16),
            pltpu.VMEM((6, BLOCK_D, 256), BF16),
            pltpu.VMEM((6, CHUNK, BLOCK_D), BF16),
            pltpu.VMEM((6, CHUNK, BLOCK_D), BF16),
            pltpu.VMEM((4, 128, BLOCK_D), BF16),
            pltpu.VMEM((4, 128, BLOCK_D), BF16),
            pltpu.VMEM((16, 48, 128), F32),
            pltpu.VMEM((16, 48, 128), BF16),
            pltpu.VMEM((48, tokens), BF16),
            pltpu.VMEM((48, 128), BF16),
            pltpu.VMEM((2, 32, 128), F32),
            pltpu.VMEM((2, 32, 128), F32),
            pltpu.VMEM((2, 16, 256), F32),
            pltpu.VMEM((16, 48, 512), BF16),
            pltpu.VMEM((16, 48, 512), BF16),
            pltpu.VMEM((2, 48, 512), F32),
            pltpu.VMEM((8, 128, 128), F32),
            pltpu.VMEM((8, 128, 128), F32),
            pltpu.VMEM((8, 128, 128), F32),
            pltpu.VMEM((16, 8, 128), F32),
            dma((13,)), dma((4, 8)), dma((4, 8)), dma((16,)), dma((16,)), dma((16,)), dma((16,)),
            dma((2,)), dma((16,)), dma((16,)), dma((8,)), dma((8,)), dma((8,)), dma((8,)),
            dma((16,)), dma((16,)), dma((6,)), dma((6,)), dma((4,)), dma((4,)),
        ],
        compiler_params=pltpu.CompilerParams(
            collective_id=0, has_side_effects=True, vmem_limit_bytes=60 * 1024 * 1024
        ),
        cost_estimate=pl.CostEstimate(
            flops=13_000_000_000, bytes_accessed=30_000_000, transcendentals=0
        ),
        name="exchange",
    )(grad, dlow, low, hot, x, dsel, wq, wk, wv, *pieces)


def weight_pieces(w_query, w_key, w_value):
    x = lax.axis_index("tensor") % 4
    core = lax.axis_index("dp") % 2
    w_kv = jnp.concatenate([w_key, w_value], axis=1)

    def rows(w, block, skip, count):
        return lax.dynamic_slice_in_dim(w, block * BLOCK_D + core * 1024 + skip, count, 0)

    def swap(value, axis, mask):
        pairs = [(i, i ^ mask) for i in range(lax.axis_size(axis))]
        return lax.ppermute(value, axis, pairs)

    two, three = (x + 2) % 4, 3 - x
    sent = [
        rows(w_query, x + 1 - 2 * (x % 2), 0, 1024),
        jnp.concatenate([rows(w_query, two, 0, 1024), rows(w_kv, two, 0, 512)], axis=0),
        jnp.concatenate([rows(w_query, three, 0, 1024), rows(w_kv, three, 512, 512)], axis=0),
    ]
    got = [swap(value, "tensor", mask) for value, mask in zip(sent, (1, 2, 3))]
    return got + [swap(value, "dp", 1) for value in got]


def per_device(
    x_rows, d_attn, q_saved, k_saved, v_saved, w_query, w_key, w_value, down_all, up_query, up_kv,
    tenant, doc_starts,
):
    pieces = weight_pieces(w_query, w_key, w_value)
    grad, dlow, low, hot, dsel = attention_call(
        tenant, doc_starts, q_saved, k_saved, v_saved, d_attn, x_rows, down_all, up_query, up_kv
    )
    return tuple(
        exchange_call(grad, dlow, low, hot, x_rows, dsel, w_query, w_key, w_value, pieces)
    )


def solution(mesh):
    in_specs = (
        P(("dp", "tensor"), None),
        P("dp", "tensor"),
        P("dp", "tensor"),
        P("dp", "tensor"),
        P("dp", "tensor"),
        P(None, "tensor"),
        P(None, "tensor"),
        P(None, "tensor"),
        P(),
        P(None, None, "tensor"),
        P(None, None, "tensor"),
        P("dp"),
        P("dp", None),
    )
    out_specs = (
        P(("dp", "tensor"), None),
        P(None, None, "tensor"),
        P(None, None, "tensor"),
        P(None, None, "tensor"),
    )
    return jax.shard_map(
        per_device, mesh=mesh, in_specs=in_specs, out_specs=out_specs, check_vma=False
    )
```

time: 415 us -> 233 us (0.56)
  Pallas kernels: 24.3 us -> 179 us
  matrix products: 120 us -> 0 us
  waiting for transfers between devices: 142 us -> 33 us
  blocking collectives: 95.2 us -> 0 us
  between operations: 15.3 us -> 0.85 us
  other arithmetic: 11.6 us -> 0.1 us
  local copies, waits for them, and re-layouts: 2.73 us -> 14.2 us
    pallas_call x1 -> x2, Pallas kernels: 24.3 us -> 179 us  [the longest x1 156 us: exchange_call(): pl.pallas_call(exchange_kernel, in_specs=[vmem] * 6 + [hbm] * 9, out_spec...]
    reduce_scatter x2 -> x0, waiting for transfers between devices: 142 us -> none  [the longest x1 125 us: per_device(): lax.psum_scatter((total + lax.dot_general(value_gradient_flat, w_value, c...]
    dot_general x8 -> x0, matrix products: 120 us -> none  [the longest x1 56.1 us: per_device(): lax.dot_general(query_gradient_flat, w_query, contract, preferred_element...]
    psum x2 -> x0, blocking collectives: 69.9 us -> none  [the longest x1 40.5 us: per_device(): lax.psum((square_down, square_q, square_kv), 'tensor')]
    ppermute x1 -> x6, waiting for transfers between devices: 0.01 us -> 33 us  [swap(): return lax.ppermute(value, axis, pairs)]
    all_gather x1 -> x0, blocking collectives: 25.3 us -> none  [per_device(): low_rows = lax.all_gather(low_own, 'tensor', axis=1, tiled=True)]
    unnamed x8 -> x25, local copies, waits for them, and re-layouts: 0.11 us -> 10.2 us
  transfers between devices with their start and end apart: 5 -> 6, of which waited for: 2 -> 1; matrix products, arithmetic and copies ran while one was open for 30% -> 0% of each run, Pallas kernels for 0% -> 10%
where the time goes in v2:
time: 233 us; the launch traced here: 232 us
  Pallas kernels  179 us (77%)
  waiting for transfers between devices  33 us (14%)
  local copies, waits for them, and re-layouts  14.2 us (6%)
  starting transfers between devices  5.03 us (2%)
    pallas_call x1, Pallas kernels, exchange_call(): pl.pallas_call(exchange_kernel, in_specs=[vmem] * 6 + [hbm] * 9, out_spec...  156 us
    ppermute x6, waiting for transfers between devices, swap(): return lax.ppermute(value, axis, pairs)  33 us
    pallas_call x1, Pallas kernels, attention_call(): pl.pallas_call(attention_kernel, in_specs=[smem] * 2 + [vmem] * 5 + [pl.B...  22.9 us
    unnamed x25, local copies, waits for them, and re-layouts  10.2 us
    ppermute x6, starting transfers between devices, swap(): return lax.ppermute(value, axis, pairs)  5.03 us
  transfers between devices with their start and end apart: 6, of which 1 were waited for; matrix products, arithmetic and copies ran while one was open for 0% of the time, Pallas kernels for 10%

profile of v2, /device:TPU:0, one launch (start us, length us, event | category | flops | bytes accessed | tf_op | source)
XLA Modules:
  0.0 232.5 jit_solution(18097221551217761487)
XLA Ops:
  0.7 0.0 copy-start
  0.7 3.3 %constant_dynamic-update-slice_fusion.1 = bf16[8192,256]{1,0:T(8,128)(2,1)} fusion(bf16[8192,128]{1,0:T(8,128)(2,1)} %wk_ref.1), kind=kLoop, calls=%fused_computation.3 | loop fusion | bytes 4194304
  4.0 0.0 copy-done
  4.0 1.5 constant_dynamic-update-slice_fusion
  5.6 1.1 constant_dynamic-slice_fusion
  6.6 1.5 constant_dynamic-slice_fusion.1
  8.1 0.1 pad_maximum_fusion.1
  8.2 2.9 %collective-permute-start.2 = (bf16[1536,256]{1,0:T(8,128)(2,1)S(1)}, bf16[1536,256]{1,0:T(8,128)(2,1)S(1)}, u32[]{:S(2)}, u32[]{:S(2)}) collective-permute-start(bf16[1536,256]{1,0:T(8,128)(2,1)S(1)} %pad_maximum_fusion.1), channel_id=1, source_target_pairs={{0,3},{1,2},{2,1},{3,0},{4,7},{5,6},{6,5},{7,4},{8,11},{9,10},{10,... | collective-permute-start | bytes 2359304 | tf_op jit(solution)/shard_map/ppermute | solution.py:636
  11.1 0.1 pad_maximum_fusion
  11.2 0.9 collective-permute-start.1
  12.0 0.5 collective-permute-start
  12.5 33.0 %collective-permute-done.2.p3_ref = bf16[1536,256]{1,0:T(8,128)(2,1)S(1)} collective-permute-done((bf16[1536,256]{1,0:T(8,128)(2,1)S(1)}, bf16[1536,256]{1,0:T(8,128)(2,1)S(1)}, u32[]{:S(2)}, u32[]{:S(2)}) %collective-permute-start.2) | collective-permute-done | bytes 786464 | tf_op jit(solution)/shard_map/ppermute | solution.py:636
  45.5 0.0 collective-permute-start.5
  45.5 0.0 collective-permute-done.1.p2_ref
  45.5 0.5 collective-permute-start.4
  46.0 0.0 collective-permute-done.p1_ref
  46.0 0.3 collective-permute-start.3
  46.3 22.9 %attention_back.1 = (bf16[2048,512]{1,0:T(8,128)(2,1)}, f32[16,48,128]{2,1,0:T(8,128)}, bf16[48,128]{1,0:T(8,128)(2,1)}, f32[8,128]{1,0:T(8,128)}, bf16[48,8192]{1,0:T(8,128)(2,1)}) custom-call(s32[2]{0:T(128)} %tenant_ref.1, s32[2,4]{1,0:T(2,128)} %doc_ref.1, bf16[2048,256]{1,0:T(8,128)(2,1)} %q_ref.1, bf16[2048,128]{1,0:T(8,128)(2,1)} %k_ref.1, ...), custom_call_target="tpu_custom_call" | custom-call | flops 6400000000 | bytes 10000000 | tf_op jit(solution)/shard_map/attention_back/pallas_call | solution.py:133
  69.2 0.0 copy-done.4
  69.2 0.0 copy-done.5
  69.3 0.0 copy-done.8
  69.3 0.0 collective-permute-done.3.c1_ref
  69.3 0.0 collective-permute-done.5.c3_ref
  69.3 0.0 collective-permute-done.4.c2_ref
  69.3 0.8 copy-done.9
  70.1 0.3 copy-done.6
  70.4 0.6 copy-done.7
  71.0 156.3 %exchange.1 = (bf16[128,8192]{1,0:T(8,128)(2,1)}, f32[4,48,512]{2,1,0:T(8,128)}, f32[4,16,256]{2,1,0:T(8,128)}, f32[4,32,128]{2,1,0:T(8,128)}) custom-call(bf16[2048,512]{1,0:T(8,128)(2,1)} %get-tuple-element.9.grad_ref, f32[16,48,128]{2,1,0:T(8,128)} %get-tuple-element.10.dlow_ref, bf16[48,128]{1,0:T(8,128)(2,1)} %get-tuple-element.11.low_ref, ...), custom_call_target="tpu_custom_call" | custom-call | flops 12999999488 | bytes 30000000 | tf_op jit(solution)/shard_map/exchange/pallas_call | solution.py:580
  227.3 3.1 %copy.24 = bf16[128,8192]{1,0:T(8,128)(2,1)} copy(bf16[128,8192]{1,0:T(8,128)(2,1)} %get-tuple-element.23) | data formatting | bytes 4194304
  230.5 0.7 copy.25
  231.2 0.6 copy.26
  231.8 0.6 copy.27
  (12 shorter events, 0.0 us)
Async XLA Ops:
  0.7 3.3 %copy-start = (bf16[8192,128]{1,0:T(8,128)(2,1)S(1)}, bf16[8192,128]{1,0:T(8,128)(2,1)}, u32[]{:S(2)}) copy-start(bf16[8192,128]{1,0:T(8,128)(2,1)} %wv_ref.1) | copy-start | bytes 6291460
  8.2 37.3 %collective-permute-start.2 = (bf16[1536,256]{1,0:T(8,128)(2,1)S(1)}, bf16[1536,256]{1,0:T(8,128)(2,1)S(1)}, u32[]{:S(2)}, u32[]{:S(2)}) collective-permute-start(bf16[1536,256]{1,0:T(8,128)(2,1)S(1)} %pad_maximum_fusion.1), channel_id=1, source_target_pairs={{0,3},{1,2},{2,1},{3,0},{4,7},{5,6},{6,5},{7,4},{8,11},{9,10},{10,... | collective-permute-start | bytes 2359304 | tf_op jit(solution)/shard_map/ppermute | solution.py:636
  11.2 34.3 %collective-permute-start.1 = (bf16[1536,256]{1,0:T(8,128)(2,1)S(1)}, bf16[1536,256]{1,0:T(8,128)(2,1)S(1)}, u32[]{:S(2)}, u32[]{:S(2)}) collective-permute-start(bf16[1536,256]{1,0:T(8,128)(2,1)S(1)} %pad_maximum_fusion), channel_id=1, source_target_pairs={{0,2},{1,3},{2,0},{3,1},{4,6},{5,7},{6,4},{7,5},{8,10},{9,11},{10,... | collective-permute-start | bytes 2359304 | tf_op jit(solution)/shard_map/ppermute | solution.py:636
  12.0 34.0 %collective-permute-start = (bf16[1024,256]{1,0:T(8,128)(2,1)S(1)}, bf16[1024,256]{1,0:T(8,128)(2,1)S(1)}, u32[]{:S(2)}, u32[]{:S(2)}) collective-permute-start(bf16[1024,256]{1,0:T(8,128)(2,1)S(1)} %get-tuple-element.16), channel_id=1, source_target_pairs={{0,1},{1,0},{2,3},{3,2},{4,5},{5,4},{6,7},{7,6},{8,9},{9,8},{10,11... | collective-permute-start | bytes 1572872 | tf_op jit(solution)/shard_map/ppermute | solution.py:636
  45.5 23.7 %copy-start.4 = (bf16[1536,256]{1,0:T(8,128)(2,1)}, bf16[1536,256]{1,0:T(8,128)(2,1)S(1)}, u32[]{:S(2)}) copy-start(bf16[1536,256]{1,0:T(8,128)(2,1)S(1)} %collective-permute-done.2.p3_ref) | copy-start | bytes 2359300
  45.5 23.8 %collective-permute-start.5 = (bf16[1536,256]{1,0:T(8,128)(2,1)S(1)}, bf16[1536,256]{1,0:T(8,128)(2,1)S(1)}, u32[]{:S(2)}, u32[]{:S(2)}) collective-permute-start(bf16[1536,256]{1,0:T(8,128)(2,1)S(1)} %collective-permute-done.2.p3_ref), channel_id=1, source_target_pairs={{0,16},{16,0},{32,48},{48,32},{64,80},{80,64},{96,112},{112,96},{1... | collective-permute-start | bytes 2359304 | tf_op jit(solution)/shard_map/ppermute | solution.py:636
  45.5 23.7 %copy-start.5 = (bf16[1536,256]{1,0:T(8,128)(2,1)}, bf16[1536,256]{1,0:T(8,128)(2,1)S(1)}, u32[]{:S(2)}) copy-start(bf16[1536,256]{1,0:T(8,128)(2,1)S(1)} %collective-permute-done.1.p2_ref) | copy-start | bytes 2359300
  45.5 23.8 %collective-permute-start.4 = (bf16[1536,256]{1,0:T(8,128)(2,1)S(1)}, bf16[1536,256]{1,0:T(8,128)(2,1)S(1)}, u32[]{:S(2)}, u32[]{:S(2)}) collective-permute-start(bf16[1536,256]{1,0:T(8,128)(2,1)S(1)} %collective-permute-done.1.p2_ref), channel_id=1, source_target_pairs={{0,16},{16,0},{32,48},{48,32},{64,80},{80,64},{96,112},{112,96},{1... | collective-permute-start | bytes 2359304 | tf_op jit(solution)/shard_map/ppermute | solution.py:636
  46.0 23.2 %copy-start.8 = (bf16[1024,256]{1,0:T(8,128)(2,1)}, bf16[1024,256]{1,0:T(8,128)(2,1)S(1)}, u32[]{:S(2)}) copy-start(bf16[1024,256]{1,0:T(8,128)(2,1)S(1)} %collective-permute-done.p1_ref) | copy-start | bytes 1572868
  46.0 23.2 %collective-permute-start.3 = (bf16[1024,256]{1,0:T(8,128)(2,1)S(1)}, bf16[1024,256]{1,0:T(8,128)(2,1)S(1)}, u32[]{:S(2)}, u32[]{:S(2)}) collective-permute-start(bf16[1024,256]{1,0:T(8,128)(2,1)S(1)} %collective-permute-done.p1_ref), channel_id=1, source_target_pairs={{0,16},{16,0},{32,48},{48,32},{64,80},{80,64},{96,112},{112,96},{1... | collective-permute-start | bytes 1572872 | tf_op jit(solution)/shard_map/ppermute | solution.py:636
  69.3 0.8 copy-start.9
  69.3 1.1 copy-start.6
  70.1 0.9 copy-start.7
  227.3 3.2 %copy-start.1 = (f32[4,48,512]{2,1,0:T(8,128)S(1)}, f32[4,48,512]{2,1,0:T(8,128)}, u32[]{:S(2)}) copy-start(f32[4,48,512]{2,1,0:T(8,128)} %get-tuple-element.24) | copy-start | bytes 1179652
  227.3 3.9 %copy-start.3 = (f32[4,16,256]{2,1,0:T(8,128)S(1)}, f32[4,16,256]{2,1,0:T(8,128)}, u32[]{:S(2)}) copy-start(f32[4,16,256]{2,1,0:T(8,128)} %get-tuple-element.25) | copy-start | bytes 196612
  227.3 4.5 %copy-start.2 = (f32[4,32,128]{2,1,0:T(8,128)S(1)}, f32[4,32,128]{2,1,0:T(8,128)}, u32[]{:S(2)}) copy-start(f32[4,32,128]{2,1,0:T(8,128)} %get-tuple-element.26) | copy-start | bytes 196612

commit v3 on v2

v3 whole, which is shorter than its diff:
```python
import functools
import math
import numpy as np
import jax
import jax.numpy as jnp
from jax import lax
from jax.experimental import pallas as pl
from jax.experimental.pallas import tpu as pltpu
from jax.sharding import PartitionSpec as P

HD = 128
RANK = 16
TEN = 4
SEQ = 1024
ROPE_BASE = 500000.0
NORM_EPS = 1e-06
MASKED = -1e30
NT = (((1,), (1,)), ((), ()))
TN = (((0,), (0,)), ((), ()))
F32 = jnp.float32
BF16 = jnp.bfloat16
ROWS = 256


def rope_constants():
    half = HD // 2
    freq = ROPE_BASE ** (-(2.0 * np.arange(half)) / HD)
    angle = np.arange(SEQ)[:, None] * freq[None, :]
    cosine = np.concatenate([np.cos(angle), np.cos(angle)], axis=1)
    sine = np.concatenate([np.sin(angle), -np.sin(angle)], axis=1)
    return cosine.astype(np.float32), sine.astype(np.float32)


MESH_ID = pl.DeviceIdType.MESH
CHUNK = 256
SUB = 128
QUARTER = 512
BLOCK_D = 2048
ORDER = ((2, 0), (1, 0), (3, 0), (0, 0), (2, 1), (1, 1), (3, 1), (0, 1))


def fused_kernel(
    tenant_ref, doc_ref, q_ref, k_ref, v_ref, g_ref, x_ref, down_ref, upq_ref, upkv_ref,
    cos_ref, sin_ref, wq_ref, wk_ref, wv_ref,
    out_ref, ud_ref, uq_ref, ukv_ref,
    grad_ref, dlow_ref, low_ref, hot_ref, kt_ref, vt_ref, dk_ref, dv_ref, c_ref, s_ref,
    gall, a_ref, wx, part, zbuf, fbuf, fin,
    dlall, lowall, lowcat, dlw_ref, kvown, kvpeer, qown, gdown, gdall, dsum,
    rsbuf, rsall, agbuf, sqall,
    wsem, wxsend, wxrecv, wysend, wyrecv, wcsend, wcrecv,
    gsend, grecv, dlsend, dlrecv, lowsend, lowrecv, kvsem, dnsend, dnrecv,
    rssend, rsrecv, agsend, agrecv, sqsend, sqrecv, zsend, zrecv, fsend, frecv,
):
    me_dp = lax.axis_index("dp")
    me_t = lax.axis_index("tensor")
    z = me_t // 4
    x = me_t % 4
    core = me_dp % 2
    xr, xl, xo = (x + 1) % 4, (x + 3) % 4, (x + 2) % 4
    pair = x + 1 - 2 * (x % 2)
    mirror = 3 - x
    z_right = ((z + 1) % 4) * 4 + x
    z_left = ((z + 3) % 4) * 4 + x

    def remote(src, dst, ssem, rsem, dp, t):
        return pltpu.make_async_remote_copy(
            src_ref=src, dst_ref=dst, send_sem=ssem, recv_sem=rsem,
            device_id=(dp, t), device_id_type=MESH_ID,
        )

    barrier = pltpu.get_barrier_semaphore()

    def greet_tensor(o, c):
        pl.semaphore_signal(
            barrier, inc=1, device_id=(me_dp, (me_t + o) % 16), device_id_type=MESH_ID
        )
        return c

    def greet_dp(o, c):
        pl.semaphore_signal(
            barrier, inc=1, device_id=((me_dp + o) % 8, me_t), device_id_type=MESH_ID
        )
        return c

    lax.fori_loop(1, 16, greet_tensor, 0)
    lax.fori_loop(1, 8, greet_dp, 0)

    y = me_dp // 2
    kv_here = 4 + x // 2
    kv_there = 5 - x // 2
    blocks = (pair, xo, mirror, kv_there)
    my_part = core * 1024 + y * 256
    d0 = pl.multiple_of(x * BLOCK_D, BLOCK_D)

    def rows_at(start, count):
        return pl.ds(pl.multiple_of(start, count), count)

    w_own = [
        pltpu.make_async_copy(src, dst, wsem.at[i])
        for i, (src, dst) in enumerate((
            (wq_ref.at[pl.ds(d0, BLOCK_D), :], wx.at[x]),
            (wk_ref.at[pl.ds(d0, BLOCK_D), :], wx.at[kv_here, :, pl.ds(0, 128)]),
            (wv_ref.at[pl.ds(d0, BLOCK_D), :], wx.at[kv_here, :, pl.ds(128, 128)]),
        ))
    ]

    def weights_x(sending):
        copies = []
        for i, xs in enumerate((pair, xo, mirror)):
            if sending:
                src = wq_ref.at[rows_at(xs * BLOCK_D + my_part, 256), :]
                dst = wx.at[x, rows_at(my_part, 256), :]
            else:
                src = dst = wx.at[xs, rows_at(my_part, 256), :]
            copies.append(remote(src, dst, wxsend.at[i], wxrecv.at[i], me_dp, z * 4 + xs))
        for i, xs in enumerate((xo, mirror)):
            for n, w in enumerate((wk_ref, wv_ref)):
                lanes = pl.ds(128 * n, 128)
                if sending:
                    row = my_part + (x % 2) * 128
                    src = w.at[rows_at(xs * BLOCK_D + row, 128), :]
                    dst = wx.at[kv_here, rows_at(row, 128), lanes]
                else:
                    row = my_part + (xs % 2) * 128
                    src = dst = wx.at[kv_there, rows_at(row, 128), lanes]
                k = 3 + 2 * i + n
                copies.append(remote(src, dst, wxsend.at[k], wxrecv.at[k], me_dp, z * 4 + xs))
        return copies

    def weights_y(sending):
        copies = []
        for i, b in enumerate(blocks):
            for o in range(1, 4):
                at_y = y if sending else (y + 4 - o) % 4
                ref = wx.at[b, rows_at(core * 1024 + at_y * 256, 256), :]
                to = ((y + o) % 4) * 2 + core
                copies.append(
                    remote(ref, ref, wysend.at[i, o - 1], wyrecv.at[i, o - 1], to, me_t)
                )
        return copies

    def weights_core(sending):
        copies = []
        for i, b in enumerate(blocks):
            at_core = core if sending else 1 - core
            ref = wx.at[b, rows_at(at_core * 1024, 1024), :]
            to = me_dp + 1 - 2 * core
            copies.append(remote(ref, ref, wcsend.at[i], wcrecv.at[i], to, me_t))
        return copies

    pl.semaphore_wait(barrier, 22)
    for copy in weights_x(True) + w_own:
        copy.start()

    def first_row(c):
        off, half = ORDER[c]
        return pl.multiple_of(((z + off) % 4) * QUARTER + half * CHUNK, CHUNK)

    def gather_out(c):
        rows = pl.ds(first_row(c), CHUNK)
        src = grad_ref.at[rows, :]
        dst = gall.at[x, rows, :]
        return (
            remote(src, dst, gsend.at[0, c], grecv.at[0, c], me_dp, z * 4 + xr),
            remote(src, dst, gsend.at[1, c], grecv.at[1, c], me_dp, z * 4 + xl),
        )

    def gather_in(c):
        rows = pl.ds(first_row(c), CHUNK)
        from_l = gall.at[xl, rows, :]
        from_r = gall.at[xr, rows, :]
        return (
            remote(from_l, from_l, gsend.at[0, c], grecv.at[0, c], me_dp, z * 4 + xr),
            remote(from_r, from_r, gsend.at[1, c], grecv.at[1, c], me_dp, z * 4 + xl),
        )

    def forward_out(c):
        r0 = first_row(c)
        to_r = gall.at[xl, pl.ds(r0, CHUNK // 2), :]
        to_l = gall.at[xr, pl.ds(pl.multiple_of(r0 + CHUNK // 2, CHUNK // 2), CHUNK // 2), :]
        return (
            remote(to_r, to_r, gsend.at[2, c], grecv.at[2, c], me_dp, z * 4 + xr),
            remote(to_l, to_l, gsend.at[3, c], grecv.at[3, c], me_dp, z * 4 + xl),
        )

    def forward_in(c):
        r0 = first_row(c)
        from_l = gall.at[xo, pl.ds(r0, CHUNK // 2), :]
        from_r = gall.at[xo, pl.ds(pl.multiple_of(r0 + CHUNK // 2, CHUNK // 2), CHUNK // 2), :]
        return (
            remote(from_l, from_l, gsend.at[2, c], grecv.at[2, c], me_dp, z * 4 + xr),
            remote(from_r, from_r, gsend.at[3, c], grecv.at[3, c], me_dp, z * 4 + xl),
        )

    def start(copies):
        for copy in copies:
            copy.start()

    def arrive(c):
        for copy in gather_in(c):
            copy.wait_recv()
        start(forward_out(c))

    def to_tensor(src, buf, ssem, rsem, picked):
        def descriptor(t):
            return remote(
                src.at[t] if picked else src, buf.at[me_t], ssem.at[t], rsem.at[me_t], me_dp, t
            )

        def begin(o, c):
            descriptor((me_t + o) % 16).start()
            return c

        def receive(o, c):
            t = (me_t + o) % 16
            remote(buf.at[t], buf.at[t], ssem.at[t], rsem.at[t], me_dp, t).wait_recv()
            return c

        def sent(o, c):
            descriptor((me_t + o) % 16).wait_send()
            return c

        return (
            lambda: lax.fori_loop(1, 16, begin, 0),
            lambda: lax.fori_loop(1, 16, receive, 0),
            lambda: lax.fori_loop(1, 16, sent, 0),
        )

    def to_dp(src_at, buf, ssem, rsem):
        def descriptor(d):
            return remote(src_at(d), buf.at[me_dp], ssem.at[d], rsem.at[me_dp], d, me_t)

        def begin(o, c):
            descriptor((me_dp + o) % 8).start()
            return c

        def receive(o, c):
            d = (me_dp + o) % 8
            remote(buf.at[d], buf.at[d], ssem.at[d], rsem.at[d], d, me_t).wait_recv()
            return c

        def sent(o, c):
            descriptor((me_dp + o) % 8).wait_send()
            return c

        return (
            lambda: lax.fori_loop(1, 8, begin, 0),
            lambda: lax.fori_loop(1, 8, receive, 0),
            lambda: lax.fori_loop(1, 8, sent, 0),
        )

    dl_start, dl_recv, dl_sent = to_tensor(dlow_ref, dlall, dlsend, dlrecv, True)
    low_start, low_recv, low_sent = to_tensor(low_ref, lowall, lowsend, lowrecv, False)
    dn_start, dn_recv, dn_sent = to_tensor(gdown, gdall, dnsend, dnrecv, True)
    sq_start, sq_recv, sq_sent = to_tensor(sqall.at[me_t], sqall, sqsend, sqrecv, False)
    rs_start, rs_recv, rs_sent = to_dp(lambda d: rsbuf.at[d], rsall, rssend, rsrecv)
    ag_start, ag_recv, ag_sent = to_dp(lambda d: agbuf.at[me_dp], agbuf, agsend, agrecv)
    kv_copy = remote(kvown, kvpeer, kvsem.at[0], kvsem.at[1], me_dp, z * 4 + pair)

    for s in range(2):
        for t in range(TEN):
            hot_ref[4 * s + t : 4 * s + t + 1, :] = jnp.where(
                jnp.full((1, 128), tenant_ref[s]) == t, 1.0, 0.0
            )
    own = tenant_ref[me_t // 8]
    low_ref[...] = lax.dot_general(
        down_ref[own], x_ref[...], NT, preferred_element_type=F32
    ).astype(BF16)
    low_start()

    scale = HD ** (-0.5)
    scale2 = scale * math.log2(math.e)

    def sequence(turn, carry):
        s = (1 - z // 2 + turn) % 2
        base = pl.multiple_of(s * SEQ, SEQ)
        starts = [doc_ref[s, j] for j in range(4)]
        pos = lax.broadcasted_iota(jnp.int32, (SEQ, HD), 0)
        cb = jnp.broadcast_to(cos_ref[pl.ds(starts[0], 1), :], (SEQ, HD))
        sb = jnp.broadcast_to(sin_ref[pl.ds(starts[0], 1), :], (SEQ, HD))
        for j in range(1, 4):
            inside = pos >= starts[j]
            cb = jnp.where(inside, cos_ref[pl.ds(starts[j], 1), :], cb)
            sb = jnp.where(inside, sin_ref[pl.ds(starts[j], 1), :], sb)
        cp = cos_ref[...]
        sp = sin_ref[...]
        c_ref[...] = cp * cb + sp * sb
        s_ref[...] = sp * cb - cp * sb
        kt_ref[...] = k_ref[pl.ds(base, SEQ), :].T
        vt_ref[...] = v_ref[pl.ds(base, SEQ), :].T
        dk_ref[...] = jnp.zeros_like(dk_ref)
        dv_ref[...] = jnp.zeros_like(dv_ref)
        for h in range(2):
            cols = slice(h * HD, (h + 1) * HD)
            for i in range(SEQ // ROWS):
                width = (i + 1) * ROWS
                rows = pl.ds(base + i * ROWS, ROWS)
                keys = pl.ds(base, width)
                q = q_ref[rows, cols]
                g = g_ref[rows, cols]
                p_row = lax.broadcasted_iota(jnp.int32, (1, ROWS), 1) + i * ROWS
                begin = jnp.zeros((1, ROWS), jnp.int32)
                for j in range(1, 4):
                    begin = jnp.where(p_row >= starts[j], starts[j], begin)
                k_idx = lax.broadcasted_iota(jnp.int32, (width, ROWS), 0)
                allowed = (k_idx >= begin) & (k_idx <= p_row)
                st = lax.dot_general(k_ref[keys, :], q, NT, preferred_element_type=F32)
                st = jnp.where(allowed, st * scale2, MASKED)
                top = jnp.max(st, axis=0, keepdims=True)
                e = jnp.exp2(st - top)
                inv = 1.0 / jnp.sum(e, axis=0, keepdims=True)
                p = e * inv
                p_low = p.astype(BF16)
                ot = jnp.dot(vt_ref[:, :width], p_low, preferred_element_type=F32)
                delta = jnp.sum(g.astype(F32).T * ot, axis=0, keepdims=True)
                dpt = lax.dot_general(v_ref[keys, :], g, NT, preferred_element_type=F32)
                ds_low = (p * (dpt - delta)).astype(BF16)
                dqt = jnp.dot(kt_ref[:, :width], ds_low, preferred_element_type=F32)
                dk_ref[:width, :] += jnp.dot(ds_low, q, preferred_element_type=F32)
                dv_ref[:width, :] += jnp.dot(p_low, g, preferred_element_type=F32)
                dq = dqt.T * scale
                dq = dq * c_ref[i * ROWS : (i + 1) * ROWS, :] + pltpu.roll(
                    dq, HD // 2, 1
                ) * s_ref[i * ROWS : (i + 1) * ROWS, :]
                grad_ref[rows, cols] = dq.astype(BF16)
            if h == 0:

                @pl.when(turn == 0)
                def _():
                    incoming = weights_x(False)
                    outgoing = weights_y(True)
                    for n in range(4):
                        for copy in [incoming[n]] if n < 3 else incoming[3:]:
                            copy.wait_recv()
                        start(outgoing[3 * n : 3 * n + 3])

        dk = dk_ref[...] * scale
        dk = dk * c_ref[...] + pltpu.roll(dk, HD // 2, 1) * s_ref[...]
        grad_ref[pl.ds(base, SEQ), 2 * HD : 3 * HD] = dk.astype(BF16)
        grad_ref[pl.ds(base, SEQ), 3 * HD : 4 * HD] = dv_ref[...].astype(BF16)
        t = tenant_ref[s]
        seq_rows = pl.ds(base, SEQ)
        parts = [
            (upq_ref[t], slice(0, 2 * HD)),
            (upkv_ref[t, :RANK, :], slice(2 * HD, 3 * HD)),
            (upkv_ref[t, RANK:, :], slice(3 * HD, 4 * HD)),
        ]
        for n, (up, c) in enumerate(parts):
            back = 2.0 * lax.dot_general(
                up, grad_ref[seq_rows, c], NT, preferred_element_type=F32
            )
            for b in range(8):
                dlow_ref[s * 8 + b, n * RANK : (n + 1) * RANK, :] = back[:, b * 128 : (b + 1) * 128]

        @pl.when(turn == 0)
        def _():
            start(gather_out(0))

        return carry

    lax.fori_loop(0, 2, sequence, 0)

    dl_start()
    start(gather_out(1))
    start(gather_out(2))
    dlall[me_t] = dlow_ref[me_t]
    lowall[me_t] = low_ref[...]
    gall[x] = grad_ref[...]

    def step_low():
        low_recv()
        for b in range(16):
            lowcat[:, b * 128 : (b + 1) * 128] = lowall[b]
        for s in range(2):
            rows = slice(s * SEQ, (s + 1) * SEQ)
            qown[s] = 2.0 * jnp.dot(
                lowcat[:RANK, rows], grad_ref[rows, 0:256], preferred_element_type=F32
            )
            kvown[s, :RANK, :] = 2.0 * jnp.dot(
                lowcat[RANK : 2 * RANK, rows], grad_ref[rows, 256:384], preferred_element_type=F32
            )
            kvown[s, RANK:, :] = 2.0 * jnp.dot(
                lowcat[2 * RANK :, rows], grad_ref[rows, 384:512], preferred_element_type=F32
            )
        kv_copy.start()

    def step_dlow():
        dl_recv()
        total = dlall[0]
        for b in range(1, 16):
            total = total + dlall[b]
        dlw_ref[...] = total.astype(BF16)

        def column(t, c):
            gdown[t] = jnp.dot(
                dlw_ref[...], x_ref[:, pl.ds(pl.multiple_of(t * 512, 512), 512)],
                preferred_element_type=F32,
            ).astype(BF16)
            return c

        lax.fori_loop(0, 16, column, 0)
        dn_start()
        gdall[me_t] = gdown[me_t]

    def step_down():
        dn_recv()
        kv_copy.wait_recv()
        for s in range(2):
            total = gdall[8 * s].astype(F32)
            for b in range(1, 8):
                total = total + gdall[8 * s + b].astype(F32)
            dsum[s] = total
            kvown_sum = kvown[s] + kvpeer[s]
            kvpeer[s] = kvown_sum
        for j in range(8):
            cb = j % 4
            for i in range(2):
                t = 2 * (j // 4) + i
                rsbuf[j, 48 * i : 48 * (i + 1), :] = (
                    dsum[0, :, cb * 128 : (cb + 1) * 128] * hot_ref[t : t + 1, :]
                    + dsum[1, :, cb * 128 : (cb + 1) * 128] * hot_ref[4 + t : 5 + t, :]
                )
            t = j // 2
            c = j % 2
            rsbuf[j, 96:112, :] = (
                qown[0, :, c * 128 : (c + 1) * 128] * hot_ref[t : t + 1, :]
                + qown[1, :, c * 128 : (c + 1) * 128] * hot_ref[4 + t : 5 + t, :]
            )
            rsbuf[j, 112:128, :] = (
                kvpeer[0, c * 16 : (c + 1) * 16, :] * hot_ref[t : t + 1, :]
                + kvpeer[1, c * 16 : (c + 1) * 16, :] * hot_ref[4 + t : 5 + t, :]
            )
        rs_start()
        rsall[me_dp] = rsbuf[me_dp]

    def step_reduce():
        rs_recv()
        total = rsall[0]
        for b in range(1, 8):
            total = total + rsall[b]
        agbuf[me_dp] = total
        ag_start()

    def parts_of(t):
        for n in range(3):
            lo = (t % 2) * 48 + n * 16
            yield [(t // 2) * 4 + cb for cb in range(4)], slice(lo, lo + 16)
        yield [2 * t, 2 * t + 1], slice(96, 112)
        yield [2 * t], slice(112, 128)
        yield [2 * t + 1], slice(112, 128)

    def step_squares():
        ag_recv()
        row = lax.broadcasted_iota(jnp.int32, (8, 128), 0)
        lane = lax.broadcasted_iota(jnp.int32, (8, 128), 1)
        tile = jnp.zeros((8, 128), F32)
        for t in range(TEN):
            for n, (pieces, rows) in enumerate(parts_of(t)):
                total = None
                for j in pieces:
                    v = agbuf[j, rows, :]
                    total = v * v if total is None else total + v * v
                value = jnp.sum(
                    jnp.sum(total, axis=0, keepdims=True), axis=1, keepdims=True
                )
                tile = jnp.where((row == t) & (lane == n), value, tile)
        sqall[me_t] = tile
        sq_start()

    def step_update():
        sq_recv()
        total = sqall[0]
        for b in range(1, 16):
            total = total + sqall[b]
        for t in range(TEN):
            for n, (pieces, rows) in enumerate(parts_of(t)):
                count = RANK * (8192 if n < 3 else 4096 if n == 3 else 2048)
                factor = 1.0 / jnp.sqrt(total[t : t + 1, n : n + 1] * (1.0 / count) + NORM_EPS)
                for i, j in enumerate(pieces):
                    value = agbuf[j, rows, :] * factor
                    if n < 3:
                        ud_ref[t, n * 16 : (n + 1) * 16, i * 128 : (i + 1) * 128] = value
                    elif n == 3:
                        uq_ref[t, :, i * 128 : (i + 1) * 128] = value
                    else:
                        ukv_ref[t, (n - 4) * 16 : (n - 3) * 16, :] = value

    def product(c, write, added):
        rows = pl.ds(first_row(c), CHUNK)
        for b in range(4):
            a_ref[b] = gall[b, rows, 0:256]
        for b in range(2):
            a_ref[4 + b] = (
                gall[2 * b, rows, 256:512].astype(F32) + gall[2 * b + 1, rows, 256:512].astype(F32)
            ).astype(BF16)

        def tile(n, carry):
            cols = pl.ds(pl.multiple_of(n * 512, 512), 512)
            acc = lax.dot_general(a_ref[0], wx[0, cols, :], NT, preferred_element_type=F32)
            for b in range(1, 6):
                acc = acc + lax.dot_general(
                    a_ref[b], wx[b, cols, :], NT, preferred_element_type=F32
                )
            write(cols, acc, added)
            return carry

        lax.fori_loop(0, 4, tile, 0)

    def z_copy(h, side, n):
        return remote(
            part.at[h, side, n], zbuf.at[h, side, n], zsend.at[h, side, n], zrecv.at[h, side, n],
            me_dp, z_left if side else z_right,
        )

    def to_far(h):
        def write(cols, acc, added):
            part[h, 0, 0, :, cols] = acc[:SUB].astype(BF16)
            part[h, 1, 0, :, cols] = acc[SUB:].astype(BF16)

        return write

    def to_near(h, side):
        def write(cols, acc, added):
            part[h, side, 2 - side, :, cols] = acc[:SUB].astype(BF16)
            part[h, side, 1 + side, :, cols] = acc[SUB:].astype(BF16)

        return write

    def to_final(h):
        def write(cols, acc, added):
            for i in range(2):
                total = acc[i * SUB : (i + 1) * SUB]
                for ref in added[i]:
                    total = total + ref[:, cols].astype(F32)
                fbuf[2 * h + i, :, cols] = total.astype(BF16)

        return write

    def add_far(h, side):
        z_copy(h, side, 0).wait_recv()
        for n in range(4):
            cols = slice(n * 512, (n + 1) * 512)
            part[h, side, 2, :, cols] = (
                part[h, side, 2, :, cols].astype(F32) + zbuf[h, side, 0, :, cols].astype(F32)
            ).astype(BF16)
        z_copy(h, side, 2).start()

    def final_copy(o):
        return remote(fbuf.at[o], fin.at[x], fsend.at[o], frecv.at[x], me_dp, z * 4 + o)

    def finish(c):
        h = ORDER[c][1]
        for side in range(2):
            for n in (1, 2):
                z_copy(h, side, n).wait_recv()
        product(
            c, to_final(h),
            ((zbuf.at[h, 0, 2], zbuf.at[h, 1, 1]), (zbuf.at[h, 0, 1], zbuf.at[h, 1, 2])),
        )
        for o in (2 * h, 2 * h + 1):

            @pl.when(x != o)
            def _(o=o):
                final_copy(o).start()

    def step_output():
        for n in range(16):
            cols = slice(n * 512, (n + 1) * 512)
            out_ref[:, cols] = lax.dot_general(
                dlw_ref[...], down_ref[own, :, cols], TN, preferred_element_type=F32
            ).astype(BF16)

    def ready(c):
        for copy in forward_in(c):
            copy.wait_recv()

    arrive(0)
    start(gather_out(3))
    step_dlow()
    incoming = weights_y(False)
    outgoing = weights_core(True)
    for n in range(4):
        for copy in incoming[3 * n : 3 * n + 3]:
            copy.wait_recv()
        outgoing[n].start()
    arrive(1)
    start(gather_out(4))
    for copy in w_own:
        copy.wait()
    for copy in weights_core(False):
        copy.wait_recv()
    for h in range(2):
        c = 4 * h
        ready(c)
        product(c, to_far(h), None)
        z_copy(h, 0, 0).start()
        z_copy(h, 1, 0).start()
        for side in range(2):
            arrive(c + 2 + side)
            if c + 5 + side < 8:
                start(gather_out(c + 5 + side))
            ready(c + 1 + side)
            product(c + 1 + side, to_near(h, side), None)
            z_copy(h, side, 1).start()
        (step_low, step_reduce)[h]()
        add_far(h, 0)
        add_far(h, 1)
        if h == 0:
            arrive(4)
            start(gather_out(7))
            step_down()
            arrive(5)
            step_output()
        else:
            step_squares()
        ready(c + 3)
        finish(c + 3)

    step_update()
    fin[x] = fbuf[x]
    for o in range(1, 4):
        xs = (x + o) % 4
        remote(fin.at[xs], fin.at[xs], fsend.at[xs], frecv.at[xs], me_dp, z * 4 + xs).wait_recv()
    for b in range(4):
        cols = slice(b * BLOCK_D, (b + 1) * BLOCK_D)
        out_ref[:, cols] = (fin[b].astype(F32) + out_ref[:, cols].astype(F32)).astype(BF16)

    for c in range(8):
        for copy in gather_out(c) + forward_out(c):
            copy.wait_send()
    for copy in weights_x(True) + weights_y(True) + weights_core(True):
        copy.wait_send()
    for sent in (dl_sent, low_sent, dn_sent, sq_sent, rs_sent, ag_sent):
        sent()
    kv_copy.wait_send()
    for h in range(2):
        for side in range(2):
            for n in range(3):
                z_copy(h, side, n).wait_send()
    for o in range(4):

        @pl.when(x != o)
        def _(o=o):
            final_copy(o).wait_send()


def fused_call(tenant, docs, q, k, v, g, x, down, upq, upkv, wq, wk, wv):
    vmem = pl.BlockSpec(memory_space=pltpu.VMEM)
    smem = pl.BlockSpec(memory_space=pltpu.SMEM)
    hbm = pl.BlockSpec(memory_space=pl.ANY)
    dma = pltpu.SemaphoreType.DMA
    tokens = q.shape[0]
    cosine, sine = rope_constants()
    return pl.pallas_call(
        fused_kernel,
        in_specs=[smem] * 2 + [vmem] * 10 + [hbm] * 3,
        out_specs=[vmem] * 4,
        out_shape=[
            jax.ShapeDtypeStruct(x.shape, BF16),
            jax.ShapeDtypeStruct((TEN, 48, 512), F32),
            jax.ShapeDtypeStruct((TEN, RANK, 256), F32),
            jax.ShapeDtypeStruct((TEN, 2 * RANK, 128), F32),
        ],
        scratch_shapes=[
            pltpu.VMEM((tokens, 512), BF16),
            pltpu.VMEM((16, 48, 128), F32),
            pltpu.VMEM((48, 128), BF16),
            pltpu.VMEM((8, 128), F32),
            pltpu.VMEM((HD, SEQ), BF16), pltpu.VMEM((HD, SEQ), BF16),
            pltpu.VMEM((SEQ, HD), F32), pltpu.VMEM((SEQ, HD), F32),
            pltpu.VMEM((SEQ, HD), F32), pltpu.VMEM((SEQ, HD), F32),
            pltpu.VMEM((4, tokens, 512), BF16),
            pltpu.VMEM((6, CHUNK, 256), BF16),
            pltpu.VMEM((6, BLOCK_D, 256), BF16),
            pltpu.VMEM((2, 2, 3, SUB, BLOCK_D), BF16),
            pltpu.VMEM((2, 2, 3, SUB, BLOCK_D), BF16),
            pltpu.VMEM((4, SUB, BLOCK_D), BF16),
            pltpu.VMEM((4, SUB, BLOCK_D), BF16),
            pltpu.VMEM((16, 48, 128), F32),
            pltpu.VMEM((16, 48, 128), BF16),
            pltpu.VMEM((48, tokens), BF16),
            pltpu.VMEM((48, 128), BF16),
            pltpu.VMEM((2, 32, 128), F32),
            pltpu.VMEM((2, 32, 128), F32),
            pltpu.VMEM((2, 16, 256), F32),
            pltpu.VMEM((16, 48, 512), BF16),
            pltpu.VMEM((16, 48, 512), BF16),
            pltpu.VMEM((2, 48, 512), F32),
            pltpu.VMEM((8, 128, 128), F32),
            pltpu.VMEM((8, 128, 128), F32),
            pltpu.VMEM((8, 128, 128), F32),
            pltpu.VMEM((16, 8, 128), F32),
            dma((3,)), dma((7,)), dma((7,)), dma((4, 3)), dma((4, 3)), dma((4,)), dma((4,)),
            dma((4, 8)), dma((4, 8)), dma((16,)), dma((16,)), dma((16,)), dma((16,)),
            dma((2,)), dma((16,)), dma((16,)), dma((8,)), dma((8,)), dma((8,)), dma((8,)),
            dma((16,)), dma((16,)), dma((2, 2, 3)), dma((2, 2, 3)), dma((4,)), dma((4,)),
        ],
        compiler_params=pltpu.CompilerParams(
            collective_id=0, has_side_effects=True, vmem_limit_bytes=63 * 1024 * 1024
        ),
        cost_estimate=pl.CostEstimate(
            flops=20_000_000_000, bytes_accessed=40_000_000, transcendentals=4_000_000
        ),
        name="exchange",
    )(tenant, docs, q, k, v, g, x, down, upq, upkv, cosine, sine, wq, wk, wv)


def per_device(
    x_rows, d_attn, q_saved, k_saved, v_saved, w_query, w_key, w_value, down_all, up_query, up_kv,
    tenant, doc_starts,
):
    return tuple(
        fused_call(
            tenant, doc_starts, q_saved, k_saved, v_saved, d_attn, x_rows, down_all, up_query,
            up_kv, w_query, w_key, w_value,
        )
    )


def solution(mesh):
    in_specs = (
        P(("dp", "tensor"), None),
        P("dp", "tensor"),
        P("dp", "tensor"),
        P("dp", "tensor"),
        P("dp", "tensor"),
        P(None, "tensor"),
        P(None, "tensor"),
        P(None, "tensor"),
        P(),
        P(None, None, "tensor"),
        P(None, None, "tensor"),
        P("dp"),
        P("dp", None),
    )
    out_specs = (
        P(("dp", "tensor"), None),
        P(None, None, "tensor"),
        P(None, None, "tensor"),
        P(None, None, "tensor"),
    )
    return jax.shard_map(
        per_device, mesh=mesh, in_specs=in_specs, out_specs=out_specs, check_vma=False
    )
```

time: 233 us -> 189 us (0.81)
  the two profiles are of different devices: /device:TPU:0 before, /device:TPU:69 now
where the time goes in v3:
time: 189 us
  Pallas kernels  183 us (97%)
  local copies, waits for them, and re-layouts  5.17 us (3%)
    pallas_call x1, Pallas kernels, fused_call(): pl.pallas_call(fused_kernel, in_specs=[smem] * 2 + [vmem] * 10 + [hbm] *...  183 us
    unnamed x10, local copies, waits for them, and re-layouts  5.17 us

profile of v3, /device:TPU:69, one launch (start us, length us, event | category | flops | bytes accessed | tf_op | source)
XLA Modules:
  0.0 188.5 jit_solution(676068395876838066)
XLA Ops:
  0.6 182.7 %exchange.1 = (bf16[128,8192]{1,0:T(8,128)(2,1)}, f32[4,48,512]{2,1,0:T(8,128)}, f32[4,16,256]{2,1,0:T(8,128)}, f32[4,32,128]{2,1,0:T(8,128)}) custom-call(s32[2]{0:T(128)} %tenant_ref.1, s32[2,4]{1,0:T(2,128)} %doc_ref.1, bf16[2048,256]{1,0:T(8,128)(2,1)} %q_ref.1, bf16[2048,128]{1,0:T(8,128)(2,1)} %k_ref.1, bf16[2048,128]{1,0:T(8,128)(2,1)} %v_ref.1, ...), custom_call_target="tpu_custom_call" | custom-call | flops 20000000000 | bytes 40000000 | tf_op jit(solution)/shard_map/exchange/pallas_call | solution.py:654
  183.3 0.0 copy-start
  183.3 0.0 copy-start.2
  183.4 0.0 copy-start.1
  183.4 3.1 %copy.23 = bf16[128,8192]{1,0:T(8,128)(2,1)} copy(bf16[128,8192]{1,0:T(8,128)(2,1)} %get-tuple-element.8) | data formatting | bytes 4194304
  186.5 0.0 copy-done
  186.5 0.7 copy.24
  187.3 0.0 copy-done.2
  187.3 0.6 copy.25
  187.9 0.0 copy-done.1
  187.9 0.6 copy.26
Async XLA Ops:
  183.3 3.2 %copy-start = (f32[4,48,512]{2,1,0:T(8,128)S(1)}, f32[4,48,512]{2,1,0:T(8,128)}, u32[]{:S(2)}) copy-start(f32[4,48,512]{2,1,0:T(8,128)} %get-tuple-element.9) | copy-start | bytes 1179652
  183.3 3.9 %copy-start.2 = (f32[4,16,256]{2,1,0:T(8,128)S(1)}, f32[4,16,256]{2,1,0:T(8,128)}, u32[]{:S(2)}) copy-start(f32[4,16,256]{2,1,0:T(8,128)} %get-tuple-element.10) | copy-start | bytes 196612
  183.4 4.5 %copy-start.1 = (f32[4,32,128]{2,1,0:T(8,128)S(1)}, f32[4,32,128]{2,1,0:T(8,128)}, u32[]{:S(2)}) copy-start(f32[4,32,128]{2,1,0:T(8,128)} %get-tuple-element.11) | copy-start | bytes 196612

commit v4 on v3

--- a/solution.py
+++ b/solution.py
@@ -36,17 +36,17 @@
 SUB = 128
 QUARTER = 512
 BLOCK_D = 2048
-ORDER = ((2, 0), (1, 0), (3, 0), (0, 0), (2, 1), (1, 1), (3, 1), (0, 1))
+ORDER = ((2, 0), (1, 0), (3, 0), (2, 1), (1, 1), (3, 1), (0, 0), (0, 1))
 
 
 def fused_kernel(
-    tenant_ref, doc_ref, q_ref, k_ref, v_ref, g_ref, x_ref, down_ref, upq_ref, upkv_ref,
+    tenant_ref, doc_ref, q_ref, k_ref, v_ref, g_ref, x_hbm, down_hbm, upq_ref, upkv_ref,
     cos_ref, sin_ref, wq_ref, wk_ref, wv_ref,
     out_ref, ud_ref, uq_ref, ukv_ref,
     grad_ref, dlow_ref, low_ref, hot_ref, kt_ref, vt_ref, dk_ref, dv_ref, c_ref, s_ref,
-    gall, a_ref, wx, part, zbuf, fbuf, fin,
+    qall, kvs, kvp, kvm, wx, part, zbuf, own_ref, fbuf, fin,
     dlall, lowall, lowcat, dlw_ref, kvown, kvpeer, qown, gdown, gdall, dsum,
-    rsbuf, rsall, agbuf, sqall,
+    rsbuf, rsall, agbuf, sqall, x_ref, down_ref,
     wsem, wxsend, wxrecv, wysend, wyrecv, wcsend, wcrecv,
     gsend, grecv, dlsend, dlrecv, lowsend, lowrecv, kvsem, dnsend, dnrecv,
     rssend, rsrecv, agsend, agrecv, sqsend, sqrecv, zsend, zrecv, fsend, frecv,
@@ -56,7 +56,7 @@
     z = me_t // 4
     x = me_t % 4
     core = me_dp % 2
-    xr, xl, xo = (x + 1) % 4, (x + 3) % 4, (x + 2) % 4
+    xo = (x + 2) % 4
     pair = x + 1 - 2 * (x % 2)
     mirror = 3 - x
     z_right = ((z + 1) % 4) * 4 + x
@@ -101,6 +101,8 @@
             (wq_ref.at[pl.ds(d0, BLOCK_D), :], wx.at[x]),
             (wk_ref.at[pl.ds(d0, BLOCK_D), :], wx.at[kv_here, :, pl.ds(0, 128)]),
             (wv_ref.at[pl.ds(d0, BLOCK_D), :], wx.at[kv_here, :, pl.ds(128, 128)]),
+            (x_hbm, x_ref),
+            (down_hbm, down_ref),
         ))
     ]
 
@@ -142,10 +144,12 @@
     def weights_core(sending):
         copies = []
         for i, b in enumerate(blocks):
-            at_core = core if sending else 1 - core
-            ref = wx.at[b, rows_at(at_core * 1024, 1024), :]
-            to = me_dp + 1 - 2 * core
-            copies.append(remote(ref, ref, wcsend.at[i], wcrecv.at[i], to, me_t))
+            for o in range(4):
+                at_y = (y + 4 - o) % 4
+                at_core = core if sending else 1 - core
+                ref = wx.at[b, rows_at(at_core * 1024 + at_y * 256, 256), :]
+                to = me_dp + 1 - 2 * core
+                copies.append(remote(ref, ref, wcsend.at[i, o], wcrecv.at[i, o], to, me_t))
         return copies
 
     pl.semaphore_wait(barrier, 22)
@@ -156,41 +160,42 @@
         off, half = ORDER[c]
         return pl.multiple_of(((z + off) % 4) * QUARTER + half * CHUNK, CHUNK)
 
+    def gather(c, n, src, dst, to):
+        return remote(src, dst, gsend.at[n, c], grecv.at[n, c], me_dp, z * 4 + to)
+
     def gather_out(c):
         rows = pl.ds(first_row(c), CHUNK)
-        src = grad_ref.at[rows, :]
-        dst = gall.at[x, rows, :]
+        mine = qall.at[x, rows, :]
         return (
-            remote(src, dst, gsend.at[0, c], grecv.at[0, c], me_dp, z * 4 + xr),
-            remote(src, dst, gsend.at[1, c], grecv.at[1, c], me_dp, z * 4 + xl),
+            gather(c, 0, mine, mine, pair),
+            gather(c, 2, mine, mine, mirror),
+            gather(c, 1, kvs.at[rows, :], kvp.at[rows, :], pair),
         )
 
     def gather_in(c):
         rows = pl.ds(first_row(c), CHUNK)
-        from_l = gall.at[xl, rows, :]
-        from_r = gall.at[xr, rows, :]
+        refs = (qall.at[pair, rows, :], qall.at[mirror, rows, :], kvp.at[rows, :])
+        return [gather(c, n, ref, ref, to) for n, ref, to in zip((0, 2, 1), refs, (pair, mirror, pair))]
+
+    def half_rows(c, n):
+        return pl.ds(pl.multiple_of(first_row(c) + n * SUB, SUB), SUB)
+
+    def forward_out(c):
+        to_pair = qall.at[mirror, half_rows(c, 0), :]
+        to_mirror = qall.at[pair, half_rows(c, 1), :]
+        summed = kvm.at[x // 2, pl.ds(first_row(c), CHUNK), :]
         return (
-            remote(from_l, from_l, gsend.at[0, c], grecv.at[0, c], me_dp, z * 4 + xr),
-            remote(from_r, from_r, gsend.at[1, c], grecv.at[1, c], me_dp, z * 4 + xl),
-        )
-
-    def forward_out(c):
-        r0 = first_row(c)
-        to_r = gall.at[xl, pl.ds(r0, CHUNK // 2), :]
-        to_l = gall.at[xr, pl.ds(pl.multiple_of(r0 + CHUNK // 2, CHUNK // 2), CHUNK // 2), :]
-        return (
-            remote(to_r, to_r, gsend.at[2, c], grecv.at[2, c], me_dp, z * 4 + xr),
-            remote(to_l, to_l, gsend.at[3, c], grecv.at[3, c], me_dp, z * 4 + xl),
+            gather(c, 3, to_pair, to_pair, pair),
+            gather(c, 4, to_mirror, to_mirror, mirror),
+            gather(c, 5, summed, summed, mirror),
         )
 
     def forward_in(c):
-        r0 = first_row(c)
-        from_l = gall.at[xo, pl.ds(r0, CHUNK // 2), :]
-        from_r = gall.at[xo, pl.ds(pl.multiple_of(r0 + CHUNK // 2, CHUNK // 2), CHUNK // 2), :]
-        return (
-            remote(from_l, from_l, gsend.at[2, c], grecv.at[2, c], me_dp, z * 4 + xr),
-            remote(from_r, from_r, gsend.at[3, c], grecv.at[3, c], me_dp, z * 4 + xl),
-        )
+        refs = (
+            qall.at[xo, half_rows(c, 0), :], qall.at[xo, half_rows(c, 1), :],
+            kvm.at[1 - x // 2, pl.ds(first_row(c), CHUNK), :],
+        )
+        return [gather(c, 3 + n, ref, ref, to) for n, (ref, to) in enumerate(zip(refs, (pair, mirror, mirror)))]
 
     def start(copies):
         for copy in copies:
@@ -199,7 +204,12 @@
     def arrive(c):
         for copy in gather_in(c):
             copy.wait_recv()
-        start(forward_out(c))
+        rows = pl.ds(first_row(c), CHUNK)
+        outgoing = forward_out(c)
+        outgoing[0].start()
+        outgoing[1].start()
+        kvm[x // 2, rows, :] = (kvs[rows, :].astype(F32) + kvp[rows, :].astype(F32)).astype(BF16)
+        outgoing[2].start()
 
     def to_tensor(src, buf, ssem, rsem, picked):
         def descriptor(t):
@@ -263,10 +273,6 @@
                 jnp.full((1, 128), tenant_ref[s]) == t, 1.0, 0.0
             )
     own = tenant_ref[me_t // 8]
-    low_ref[...] = lax.dot_general(
-        down_ref[own], x_ref[...], NT, preferred_element_type=F32
-    ).astype(BF16)
-    low_start()
 
     scale = HD ** (-0.5)
     scale2 = scale * math.log2(math.e)
@@ -322,22 +328,31 @@
                 dq = dq * c_ref[i * ROWS : (i + 1) * ROWS, :] + pltpu.roll(
                     dq, HD // 2, 1
                 ) * s_ref[i * ROWS : (i + 1) * ROWS, :]
-                grad_ref[rows, cols] = dq.astype(BF16)
+                dq = dq.astype(BF16)
+                grad_ref[rows, cols] = dq
+                for n in range(4):
+                    at = (i // 2) * QUARTER + (n % 2) * CHUNK + (2 * (i % 2) + n // 2) * 64
+                    qall[x, pl.ds(base + at, 64), cols] = dq[n * 64 : (n + 1) * 64]
             if h == 0:
 
                 @pl.when(turn == 0)
                 def _():
                     incoming = weights_x(False)
                     outgoing = weights_y(True)
+                    relayed = weights_core(True)
                     for n in range(4):
                         for copy in [incoming[n]] if n < 3 else incoming[3:]:
                             copy.wait_recv()
                         start(outgoing[3 * n : 3 * n + 3])
+                        relayed[4 * n].start()
 
         dk = dk_ref[...] * scale
         dk = dk * c_ref[...] + pltpu.roll(dk, HD // 2, 1) * s_ref[...]
-        grad_ref[pl.ds(base, SEQ), 2 * HD : 3 * HD] = dk.astype(BF16)
-        grad_ref[pl.ds(base, SEQ), 3 * HD : 4 * HD] = dv_ref[...].astype(BF16)
+        for n, value in enumerate((dk.astype(BF16), dv_ref[...].astype(BF16))):
+            grad_ref[pl.ds(base, SEQ), (2 + n) * HD : (3 + n) * HD] = value
+            for b in range(16):
+                at = (b // 8) * QUARTER + (b % 2) * CHUNK + (b % 8) // 2 * 64
+                kvs[pl.ds(base + at, 64), n * HD : (n + 1) * HD] = value[b * 64 : (b + 1) * 64]
         t = tenant_ref[s]
         seq_rows = pl.ds(base, SEQ)
         parts = [
@@ -360,12 +375,17 @@
 
     lax.fori_loop(0, 2, sequence, 0)
 
-    dl_start()
     start(gather_out(1))
     start(gather_out(2))
+    dl_start()
     dlall[me_t] = dlow_ref[me_t]
+    w_own[3].wait()
+    w_own[4].wait()
+    low_ref[...] = lax.dot_general(
+        down_ref[own], x_ref[...], NT, preferred_element_type=F32
+    ).astype(BF16)
+    low_start()
     lowall[me_t] = low_ref[...]
-    gall[x] = grad_ref[...]
 
     def step_low():
         low_recv()
@@ -485,83 +505,124 @@
                     else:
                         ukv_ref[t, (n - 4) * 16 : (n - 3) * 16, :] = value
 
-    def product(c, write, added):
+    def product(c, write):
         rows = pl.ds(first_row(c), CHUNK)
-        for b in range(4):
-            a_ref[b] = gall[b, rows, 0:256]
-        for b in range(2):
-            a_ref[4 + b] = (
-                gall[2 * b, rows, 256:512].astype(F32) + gall[2 * b + 1, rows, 256:512].astype(F32)
-            ).astype(BF16)
-
         def tile(n, carry):
             cols = pl.ds(pl.multiple_of(n * 512, 512), 512)
-            acc = lax.dot_general(a_ref[0], wx[0, cols, :], NT, preferred_element_type=F32)
-            for b in range(1, 6):
-                acc = acc + lax.dot_general(
-                    a_ref[b], wx[b, cols, :], NT, preferred_element_type=F32
-                )
-            write(cols, acc, added)
+            acc = None
+            for b in range(6):
+                left = qall[b, rows, :] if b < 4 else kvm[b - 4, rows, :]
+                term = lax.dot_general(left, wx[b, cols, :], NT, preferred_element_type=F32)
+                acc = term if acc is None else acc + term
+            write(cols, acc)
             return carry
 
         lax.fori_loop(0, 4, tile, 0)
 
     def z_copy(h, side, n):
+        if n < 2:
+            src, dst = part.at[h, side, n], zbuf.at[h, side, n]
+        else:
+            cols = pl.ds((n - 2) * 1024, 1024)
+            src, dst = part.at[h, side, 2, :, cols], zbuf.at[h, side, 2, :, cols]
         return remote(
-            part.at[h, side, n], zbuf.at[h, side, n], zsend.at[h, side, n], zrecv.at[h, side, n],
+            src, dst, zsend.at[h, side, n], zrecv.at[h, side, n],
             me_dp, z_left if side else z_right,
         )
 
     def to_far(h):
-        def write(cols, acc, added):
+        def write(cols, acc):
             part[h, 0, 0, :, cols] = acc[:SUB].astype(BF16)
             part[h, 1, 0, :, cols] = acc[SUB:].astype(BF16)
 
         return write
 
     def to_near(h, side):
-        def write(cols, acc, added):
+        def write(cols, acc):
             part[h, side, 2 - side, :, cols] = acc[:SUB].astype(BF16)
             part[h, side, 1 + side, :, cols] = acc[SUB:].astype(BF16)
 
         return write
 
-    def to_final(h):
-        def write(cols, acc, added):
-            for i in range(2):
-                total = acc[i * SUB : (i + 1) * SUB]
-                for ref in added[i]:
-                    total = total + ref[:, cols].astype(F32)
-                fbuf[2 * h + i, :, cols] = total.astype(BF16)
-
-        return write
+    def write_own(cols, acc):
+        own_ref[0, :, cols] = acc[:SUB].astype(BF16)
+        own_ref[1, :, cols] = acc[SUB:].astype(BF16)
+
+    def far(h):
+        product(3 * h, to_far(h))
+        z_copy(h, 0, 0).start()
+        z_copy(h, 1, 0).start()
+
+    def near(h, side):
+        product(3 * h + 1 + side, to_near(h, side))
+        z_copy(h, side, 1).start()
 
     def add_far(h, side):
         z_copy(h, side, 0).wait_recv()
-        for n in range(4):
-            cols = slice(n * 512, (n + 1) * 512)
-            part[h, side, 2, :, cols] = (
-                part[h, side, 2, :, cols].astype(F32) + zbuf[h, side, 0, :, cols].astype(F32)
-            ).astype(BF16)
-        z_copy(h, side, 2).start()
-
-    def final_copy(o):
-        return remote(fbuf.at[o], fin.at[x], fsend.at[o], frecv.at[x], me_dp, z * 4 + o)
-
-    def finish(c):
-        h = ORDER[c][1]
+        for m in range(2):
+            for n in range(2):
+                cols = slice(m * 1024 + n * 512, m * 1024 + (n + 1) * 512)
+                part[h, side, 2, :, cols] = (
+                    part[h, side, 2, :, cols].astype(F32) + zbuf[h, side, 0, :, cols].astype(F32)
+                ).astype(BF16)
+            z_copy(h, side, 2 + m).start()
+
+    def final_copy(o, h, m):
+        rows, cols = pl.ds(h * 64, 64), pl.ds(m * 1024, 1024)
+        return remote(
+            fbuf.at[o, rows, cols], fin.at[x, rows, cols], fsend.at[o, h, m], frecv.at[x, h, m],
+            me_dp, z * 4 + o,
+        )
+
+    def finish(h):
+        for m in range(2):
+            for side in range(2):
+                if m == 0:
+                    z_copy(h, side, 1).wait_recv()
+                z_copy(h, side, 2 + m).wait_recv()
+            for i in range(2):
+                for n in range(2):
+                    cols = slice(m * 1024 + n * 512, m * 1024 + (n + 1) * 512)
+                    total = (
+                        own_ref[i, :, cols].astype(F32)
+                        + zbuf[h, 0, 2 - i, :, cols].astype(F32)
+                        + zbuf[h, 1, 1 + i, :, cols].astype(F32)
+                    ).astype(BF16)
+                    fbuf[2 * i, h * 64 : (h + 1) * 64, cols] = total[:64]
+                    fbuf[2 * i + 1, h * 64 : (h + 1) * 64, cols] = total[64:]
+                for o in (2 * i, 2 * i + 1):
+
+                    @pl.when(x != o)
+                    def _(o=o, m=m):
+                        final_copy(o, h, m).start()
+
+    def deliver(h):
+        rows = slice(h * 64, (h + 1) * 64)
+        fin[x, rows, :] = fbuf[x, rows, :]
+        for m in range(2):
+            for o in range(1, 4):
+                xs = (x + o) % 4
+                block = fin.at[xs, pl.ds(h * 64, 64), pl.ds(m * 1024, 1024)]
+                remote(
+                    block, block, fsend.at[xs, h, m], frecv.at[xs, h, m], me_dp, z * 4 + xs
+                ).wait_recv()
+            for b in range(4):
+                cols = slice(b * BLOCK_D + m * 1024, b * BLOCK_D + (m + 1) * 1024)
+                out_ref[rows, cols] = (
+                    fin[b, rows, m * 1024 : (m + 1) * 1024].astype(F32)
+                    + out_ref[rows, cols].astype(F32)
+                ).astype(BF16)
+
+    def all_sent(h):
         for side in range(2):
-            for n in (1, 2):
-                z_copy(h, side, n).wait_recv()
-        product(
-            c, to_final(h),
-            ((zbuf.at[h, 0, 2], zbuf.at[h, 1, 1]), (zbuf.at[h, 0, 1], zbuf.at[h, 1, 2])),
-        )
-        for o in (2 * h, 2 * h + 1):
+            for n in range(4):
+                z_copy(h, side, n).wait_send()
+        for o in range(4):
 
             @pl.when(x != o)
             def _(o=o):
-                final_copy(o).start()
+                final_copy(o, h, 0).wait_send()
+                final_copy(o, h, 1).wait_send()
 
     def step_output():
         for n in range(16):
@@ -576,72 +637,69 @@
 
     arrive(0)
     start(gather_out(3))
-    step_dlow()
     incoming = weights_y(False)
-    outgoing = weights_core(True)
+    relayed = weights_core(True)
     for n in range(4):
-        for copy in incoming[3 * n : 3 * n + 3]:
-            copy.wait_recv()
-        outgoing[n].start()
+        for o in range(3):
+            incoming[3 * n + o].wait_recv()
+            relayed[4 * n + o + 1].start()
     arrive(1)
     start(gather_out(4))
-    for copy in w_own:
+    for copy in w_own[:3]:
         copy.wait()
     for copy in weights_core(False):
         copy.wait_recv()
-    for h in range(2):
-        c = 4 * h
-        ready(c)
-        product(c, to_far(h), None)
-        z_copy(h, 0, 0).start()
-        z_copy(h, 1, 0).start()
-        for side in range(2):
-            arrive(c + 2 + side)
-            if c + 5 + side < 8:
-                start(gather_out(c + 5 + side))
-            ready(c + 1 + side)
-            product(c + 1 + side, to_near(h, side), None)
-            z_copy(h, side, 1).start()
-        (step_low, step_reduce)[h]()
-        add_far(h, 0)
-        add_far(h, 1)
-        if h == 0:
-            arrive(4)
-            start(gather_out(7))
-            step_down()
-            arrive(5)
-            step_output()
-        else:
-            step_squares()
-        ready(c + 3)
-        finish(c + 3)
-
-    step_update()
-    fin[x] = fbuf[x]
-    for o in range(1, 4):
-        xs = (x + o) % 4
-        remote(fin.at[xs], fin.at[xs], fsend.at[xs], frecv.at[xs], me_dp, z * 4 + xs).wait_recv()
-    for b in range(4):
-        cols = slice(b * BLOCK_D, (b + 1) * BLOCK_D)
-        out_ref[:, cols] = (fin[b].astype(F32) + out_ref[:, cols].astype(F32)).astype(BF16)
-
+    ready(0)
+    far(0)
+    arrive(2)
+    start(gather_out(5))
+    ready(1)
+    near(0, 0)
+    ready(2)
+    near(0, 1)
+    arrive(3)
+    start(gather_out(6))
+    step_dlow()
+    add_far(0, 0)
+    add_far(0, 1)
+    arrive(4)
+    start(gather_out(7))
+    ready(3)
+    far(1)
+    arrive(5)
+    step_low()
+    ready(4)
+    near(1, 0)
+    ready(5)
+    near(1, 1)
+    arrive(6)
+    step_down()
+    ready(6)
+    product(6, write_own)
+    finish(0)
+    arrive(7)
+    add_far(1, 0)
+    add_far(1, 1)
+    step_reduce()
+    ready(7)
+    product(7, write_own)
+    step_output()
+    deliver(0)
+    step_squares()
     for c in range(8):
         for copy in gather_out(c) + forward_out(c):
             copy.wait_send()
     for copy in weights_x(True) + weights_y(True) + weights_core(True):
         copy.wait_send()
-    for sent in (dl_sent, low_sent, dn_sent, sq_sent, rs_sent, ag_sent):
+    for sent in (dl_sent, low_sent, dn_sent, rs_sent, ag_sent):
         sent()
     kv_copy.wait_send()
-    for h in range(2):
-        for side in range(2):
-            for n in range(3):
-                z_copy(h, side, n).wait_send()
-    for o in range(4):
-
-        @pl.when(x != o)
-        def _(o=o):
-            final_copy(o).wait_send()
+    all_sent(0)
+    step_update()
+    sq_sent()
+    finish(1)
+    deliver(1)
+    all_sent(1)
 
 
 def fused_call(tenant, docs, q, k, v, g, x, down, upq, upkv, wq, wk, wv):
@@ -653,7 +711,7 @@
     cosine, sine = rope_constants()
     return pl.pallas_call(
         fused_kernel,
-        in_specs=[smem] * 2 + [vmem] * 10 + [hbm] * 3,
+        in_specs=[smem] * 2 + [vmem] * 4 + [hbm] * 2 + [vmem] * 4 + [hbm] * 3,
         out_specs=[vmem] * 4,
         out_shape=[
             jax.ShapeDtypeStruct(x.shape, BF16),
@@ -669,11 +727,13 @@
             pltpu.VMEM((HD, SEQ), BF16), pltpu.VMEM((HD, SEQ), BF16),
             pltpu.VMEM((SEQ, HD), F32), pltpu.VMEM((SEQ, HD), F32),
             pltpu.VMEM((SEQ, HD), F32), pltpu.VMEM((SEQ, HD), F32),
-            pltpu.VMEM((4, tokens, 512), BF16),
-            pltpu.VMEM((6, CHUNK, 256), BF16),
+            pltpu.VMEM((4, tokens, 256), BF16),
+            pltpu.VMEM((tokens, 256), BF16), pltpu.VMEM((tokens, 256), BF16),
+            pltpu.VMEM((2, tokens, 256), BF16),
             pltpu.VMEM((6, BLOCK_D, 256), BF16),
             pltpu.VMEM((2, 2, 3, SUB, BLOCK_D), BF16),
             pltpu.VMEM((2, 2, 3, SUB, BLOCK_D), BF16),
+            pltpu.VMEM((2, SUB, BLOCK_D), BF16),
             pltpu.VMEM((4, SUB, BLOCK_D), BF16),
             pltpu.VMEM((4, SUB, BLOCK_D), BF16),
             pltpu.VMEM((16, 48, 128), F32),
@@ -690,10 +750,12 @@
             pltpu.VMEM((8, 128, 128), F32),
             pltpu.VMEM((8, 128, 128), F32),
             pltpu.VMEM((16, 8, 128), F32),
-            dma((3,)), dma((7,)), dma((7,)), dma((4, 3)), dma((4, 3)), dma((4,)), dma((4,)),
-            dma((4, 8)), dma((4, 8)), dma((16,)), dma((16,)), dma((16,)), dma((16,)),
+            pltpu.VMEM(x.shape, BF16),
+            pltpu.VMEM(down.shape, BF16),
+            dma((5,)), dma((7,)), dma((7,)), dma((4, 3)), dma((4, 3)), dma((4, 4)), dma((4, 4)),
+            dma((6, 8)), dma((6, 8)), dma((16,)), dma((16,)), dma((16,)), dma((16,)),
             dma((2,)), dma((16,)), dma((16,)), dma((8,)), dma((8,)), dma((8,)), dma((8,)),
-            dma((16,)), dma((16,)), dma((2, 2, 3)), dma((2, 2, 3)), dma((4,)), dma((4,)),
+            dma((16,)), dma((16,)), dma((2, 2, 4)), dma((2, 2, 4)), dma((4, 2, 2)), dma((4, 2, 2)),
         ],
         compiler_params=pltpu.CompilerParams(
             collective_id=0, has_side_effects=True, vmem_limit_bytes=63 * 1024 * 1024

time: 189 us -> 159 us (0.84)
  the two profiles are of different devices: /device:TPU:69 before, /device:TPU:0 now
where the time goes in v4:
time: 159 us; the launch traced here: 157 us
  Pallas kernels  151 us (95%)
  local copies, waits for them, and re-layouts  5.17 us (3%)
    pallas_call x1, Pallas kernels, fused_call(): pl.pallas_call(fused_kernel, in_specs=[smem] * 2 + [vmem] * 4 + [hbm] * 2...  151 us
    unnamed x10, local copies, waits for them, and re-layouts  5.17 us

profile of v4, /device:TPU:0, one launch (start us, length us, event | category | flops | bytes accessed | tf_op | source)
XLA Modules:
  0.0 157.0 jit_solution(14215179170866819522)
XLA Ops:
  0.6 151.1 %exchange.1 = (bf16[128,8192]{1,0:T(8,128)(2,1)}, f32[4,48,512]{2,1,0:T(8,128)}, f32[4,16,256]{2,1,0:T(8,128)}, f32[4,32,128]{2,1,0:T(8,128)}) custom-call(s32[2]{0:T(128)} %tenant_ref.1, s32[2,4]{1,0:T(2,128)} %doc_ref.1, bf16[2048,256]{1,0:T(8,128)(2,1)} %q_ref.1, bf16[2048,128]{1,0:T(8,128)(2,1)} %k_ref.1, bf16[2048,128]{1,0:T(8,128)(2,1)} %v_ref.1, ...), custom_call_target="tpu_custom_call" | custom-call | flops 20000000000 | bytes 40000000 | tf_op jit(solution)/shard_map/exchange/pallas_call | solution.py:712
  151.8 0.0 copy-start
  151.8 0.0 copy-start.2
  151.8 0.0 copy-start.1
  151.8 3.1 %copy.23 = bf16[128,8192]{1,0:T(8,128)(2,1)} copy(bf16[128,8192]{1,0:T(8,128)(2,1)} %get-tuple-element.8) | data formatting | bytes 4194304
  155.0 0.0 copy-done
  155.0 0.7 copy.24
  155.7 0.0 copy-done.2
  155.7 0.6 copy.25
  156.3 0.0 copy-done.1
  156.4 0.6 copy.26
Async XLA Ops:
  151.8 3.2 %copy-start = (f32[4,48,512]{2,1,0:T(8,128)S(1)}, f32[4,48,512]{2,1,0:T(8,128)}, u32[]{:S(2)}) copy-start(f32[4,48,512]{2,1,0:T(8,128)} %get-tuple-element.9) | copy-start | bytes 1179652
  151.8 3.9 %copy-start.2 = (f32[4,16,256]{2,1,0:T(8,128)S(1)}, f32[4,16,256]{2,1,0:T(8,128)}, u32[]{:S(2)}) copy-start(f32[4,16,256]{2,1,0:T(8,128)} %get-tuple-element.10) | copy-start | bytes 196612
  151.8 4.5 %copy-start.1 = (f32[4,32,128]{2,1,0:T(8,128)S(1)}, f32[4,32,128]{2,1,0:T(8,128)}, u32[]{:S(2)}) copy-start(f32[4,32,128]{2,1,0:T(8,128)} %get-tuple-element.11) | copy-start | bytes 196612

commit v5 on v4

--- a/solution.py
+++ b/solution.py
@@ -45,10 +45,11 @@
     out_ref, ud_ref, uq_ref, ukv_ref,
     grad_ref, dlow_ref, low_ref, hot_ref, kt_ref, vt_ref, dk_ref, dv_ref, c_ref, s_ref,
     qall, kvs, kvp, kvm, wx, part, zbuf, own_ref, fbuf, fin,
-    dlall, lowall, lowcat, dlw_ref, kvown, kvpeer, qown, gdown, gdall, dsum,
+    dlx_in, dlz_out, dlz_in, lowx, lowall, lowcat, dlw_ref, kvown, kvpeer, qown,
+    gdown, dnz, dnx_out, dnx_in, dsum,
     rsbuf, rsall, agbuf, sqall, x_ref, down_ref,
     wsem, wxsend, wxrecv, wysend, wyrecv, wcsend, wcrecv,
-    gsend, grecv, dlsend, dlrecv, lowsend, lowrecv, kvsem, dnsend, dnrecv,
+    gsend, grecv, dlsend, dlrecv, esend, erecv, kvsem,
     rssend, rsrecv, agsend, agrecv, sqsend, sqrecv, zsend, zrecv, fsend, frecv,
 ):
     me_dp = lax.axis_index("dp")
@@ -259,9 +260,53 @@
             lambda: lax.fori_loop(1, 8, sent, 0),
         )
 
-    dl_start, dl_recv, dl_sent = to_tensor(dlow_ref, dlall, dlsend, dlrecv, True)
-    low_start, low_recv, low_sent = to_tensor(low_ref, lowall, lowsend, lowrecv, False)
-    dn_start, dn_recv, dn_sent = to_tensor(gdown, gdall, dnsend, dnrecv, True)
+    def to_line(along, i, src_at, buf):
+        at = x if along == "x" else z
+        peers = []
+        for o in range(1, 4):
+            p = (at + o) % 4
+            peers.append((p, z * 4 + p if along == "x" else p * 4 + x))
+
+        def out():
+            return [
+                remote(src_at(p), buf.at[at], esend.at[i, p], erecv.at[i, at], me_dp, t)
+                for p, t in peers
+            ]
+
+        def begin():
+            start(out())
+
+        def receive():
+            for p, t in peers:
+                remote(
+                    buf.at[p], buf.at[p], esend.at[i, p], erecv.at[i, p], me_dp, t
+                ).wait_recv()
+
+        def sent():
+            for copy in out():
+                copy.wait_send()
+
+        return begin, receive, sent
+
+    def dl_parts(turn, sending):
+        s = (1 - z // 2 + turn) % 2
+        copies = []
+        for o in range(1, 4):
+            p = (x + o) % 4
+            if sending:
+                src, dst = dlow_ref.at[p, pl.ds(2 * s, 2)], dlx_in.at[x, pl.ds(2 * s, 2)]
+                sems = (dlsend.at[turn, p], dlrecv.at[turn, x])
+            else:
+                src = dst = dlx_in.at[p, pl.ds(2 * s, 2)]
+                sems = (dlsend.at[turn, p], dlrecv.at[turn, p])
+            copies.append(remote(src, dst, *sems, me_dp, z * 4 + p))
+        return copies
+
+    dlz_start, dlz_recv, dlz_sent = to_line("z", 0, lambda p: dlz_out.at[p], dlz_in)
+    lowx_start, lowx_recv, lowx_sent = to_line("x", 1, lambda p: lowx.at[x], lowx)
+    lowz_start, lowz_recv, lowz_sent = to_line("z", 2, lambda p: lowx, lowall)
+    dnz_start, dnz_recv, dnz_sent = to_line("z", 3, lambda p: gdown.at[p], dnz)
+    dnx_start, dnx_recv, dnx_sent = to_line("x", 4, lambda p: dnx_out.at[p], dnx_in)
     sq_start, sq_recv, sq_sent = to_tensor(sqall.at[me_t], sqall, sqsend, sqrecv, False)
     rs_start, rs_recv, rs_sent = to_dp(lambda d: rsbuf.at[d], rsall, rssend, rsrecv)
     ag_start, ag_recv, ag_sent = to_dp(lambda d: agbuf.at[me_dp], agbuf, agsend, agrecv)
@@ -365,11 +410,21 @@
                 up, grad_ref[seq_rows, c], NT, preferred_element_type=F32
             )
             for b in range(8):
-                dlow_ref[s * 8 + b, n * RANK : (n + 1) * RANK, :] = back[:, b * 128 : (b + 1) * 128]
+                dlow_ref[b % 4, 2 * s + b // 4, n * RANK : (n + 1) * RANK, :] = back[
+                    :, b * 128 : (b + 1) * 128
+                ].astype(BF16)
+
+        start(dl_parts(turn, True))
 
         @pl.when(turn == 0)
         def _():
             start(gather_out(0))
+            w_own[3].wait()
+            w_own[4].wait()
+            lowx[x] = lax.dot_general(
+                down_ref[own], x_ref[...], NT, preferred_element_type=F32
+            ).astype(BF16)
+            lowx_start()
 
         return carry
 
@@ -377,20 +432,24 @@
 
     start(gather_out(1))
     start(gather_out(2))
-    dl_start()
-    dlall[me_t] = dlow_ref[me_t]
-    w_own[3].wait()
-    w_own[4].wait()
-    low_ref[...] = lax.dot_general(
-        down_ref[own], x_ref[...], NT, preferred_element_type=F32
+    lowx_recv()
+    lowz_start()
+    lowall[z] = lowx[...]
+    dlx_in[x] = dlow_ref[x]
+    for turn in range(2):
+        for copy in dl_parts(turn, False):
+            copy.wait_recv()
+    dlz_out[...] = (
+        (dlx_in[0].astype(F32) + dlx_in[1].astype(F32))
+        + (dlx_in[2].astype(F32) + dlx_in[3].astype(F32))
     ).astype(BF16)
-    low_start()
-    lowall[me_t] = low_ref[...]
+    dlz_start()
+    dlz_in[z] = dlz_out[z]
 
     def step_low():
-        low_recv()
+        lowz_recv()
         for b in range(16):
-            lowcat[:, b * 128 : (b + 1) * 128] = lowall[b]
+            lowcat[:, b * 128 : (b + 1) * 128] = lowall[b // 4, b % 4]
         for s in range(2):
             rows = slice(s * SEQ, (s + 1) * SEQ)
             qown[s] = 2.0 * jnp.dot(
@@ -405,30 +464,40 @@
         kv_copy.start()
 
     def step_dlow():
-        dl_recv()
-        total = dlall[0]
-        for b in range(1, 16):
-            total = total + dlall[b]
-        dlw_ref[...] = total.astype(BF16)
+        dlz_recv()
+        dlw_ref[...] = (
+            (dlz_in[0].astype(F32) + dlz_in[1].astype(F32))
+            + (dlz_in[2].astype(F32) + dlz_in[3].astype(F32))
+        ).astype(BF16)
 
         def column(t, c):
-            gdown[t] = jnp.dot(
+            gdown[t // 4, t % 4] = jnp.dot(
                 dlw_ref[...], x_ref[:, pl.ds(pl.multiple_of(t * 512, 512), 512)],
                 preferred_element_type=F32,
             ).astype(BF16)
             return c
 
         lax.fori_loop(0, 16, column, 0)
-        dn_start()
-        gdall[me_t] = gdown[me_t]
+        dnz_start()
+        dnz[z] = gdown[z]
+
+    def step_down_x():
+        dnz_recv()
+        for s in range(2):
+            for b in range(4):
+                dnx_out[b, s] = (
+                    dnz[2 * s, b].astype(F32) + dnz[2 * s + 1, b].astype(F32)
+                ).astype(BF16)
+        dnx_start()
+        dnx_in[x] = dnx_out[x]
 
     def step_down():
-        dn_recv()
+        dnx_recv()
         kv_copy.wait_recv()
         for s in range(2):
-            total = gdall[8 * s].astype(F32)
-            for b in range(1, 8):
-                total = total + gdall[8 * s + b].astype(F32)
+            total = dnx_in[0, s].astype(F32)
+            for b in range(1, 4):
+                total = total + dnx_in[b, s].astype(F32)
             dsum[s] = total
             kvown_sum = kvown[s] + kvpeer[s]
             kvpeer[s] = kvown_sum
@@ -643,6 +712,7 @@
         for o in range(3):
             incoming[3 * n + o].wait_recv()
             relayed[4 * n + o + 1].start()
+    step_dlow()
     arrive(1)
     start(gather_out(4))
     for copy in w_own[:3]:
@@ -659,15 +729,15 @@
     near(0, 1)
     arrive(3)
     start(gather_out(6))
-    step_dlow()
     add_far(0, 0)
     add_far(0, 1)
+    step_low()
     arrive(4)
     start(gather_out(7))
+    step_down_x()
     ready(3)
     far(1)
     arrive(5)
-    step_low()
     ready(4)
     near(1, 0)
     ready(5)
@@ -691,8 +761,11 @@
             copy.wait_send()
     for copy in weights_x(True) + weights_y(True) + weights_core(True):
         copy.wait_send()
-    for sent in (dl_sent, low_sent, dn_sent, rs_sent, ag_sent):
+    for sent in (dlz_sent, lowx_sent, lowz_sent, dnz_sent, dnx_sent, rs_sent, ag_sent):
         sent()
+    for turn in range(2):
+        for copy in dl_parts(turn, True):
+            copy.wait_send()
     kv_copy.wait_send()
     all_sent(0)
     step_update()
@@ -721,7 +794,7 @@
         ],
         scratch_shapes=[
             pltpu.VMEM((tokens, 512), BF16),
-            pltpu.VMEM((16, 48, 128), F32),
+            pltpu.VMEM((4, 4, 48, 128), BF16),
             pltpu.VMEM((48, 128), BF16),
             pltpu.VMEM((8, 128), F32),
             pltpu.VMEM((HD, SEQ), BF16), pltpu.VMEM((HD, SEQ), BF16),
@@ -736,15 +809,18 @@
             pltpu.VMEM((2, SUB, BLOCK_D), BF16),
             pltpu.VMEM((4, SUB, BLOCK_D), BF16),
             pltpu.VMEM((4, SUB, BLOCK_D), BF16),
-            pltpu.VMEM((16, 48, 128), F32),
-            pltpu.VMEM((16, 48, 128), BF16),
+            pltpu.VMEM((4, 4, 48, 128), BF16),
+            pltpu.VMEM((4, 48, 128), BF16), pltpu.VMEM((4, 48, 128), BF16),
+            pltpu.VMEM((4, 48, 128), BF16),
+            pltpu.VMEM((4, 4, 48, 128), BF16),
             pltpu.VMEM((48, tokens), BF16),
             pltpu.VMEM((48, 128), BF16),
             pltpu.VMEM((2, 32, 128), F32),
             pltpu.VMEM((2, 32, 128), F32),
             pltpu.VMEM((2, 16, 256), F32),
-            pltpu.VMEM((16, 48, 512), BF16),
-            pltpu.VMEM((16, 48, 512), BF16),
+            pltpu.VMEM((4, 4, 48, 512), BF16),
+            pltpu.VMEM((4, 4, 48, 512), BF16),
+            pltpu.VMEM((4, 2, 48, 512), BF16), pltpu.VMEM((4, 2, 48, 512), BF16),
             pltpu.VMEM((2, 48, 512), F32),
             pltpu.VMEM((8, 128, 128), F32),
             pltpu.VMEM((8, 128, 128), F32),
@@ -753,8 +829,8 @@
             pltpu.VMEM(x.shape, BF16),
             pltpu.VMEM(down.shape, BF16),
             dma((5,)), dma((7,)), dma((7,)), dma((4, 3)), dma((4, 3)), dma((4, 4)), dma((4, 4)),
-            dma((6, 8)), dma((6, 8)), dma((16,)), dma((16,)), dma((16,)), dma((16,)),
-            dma((2,)), dma((16,)), dma((16,)), dma((8,)), dma((8,)), dma((8,)), dma((8,)),
+            dma((6, 8)), dma((6, 8)), dma((2, 4)), dma((2, 4)), dma((5, 4)), dma((5, 4)),
+            dma((2,)), dma((8,)), dma((8,)), dma((8,)), dma((8,)),
             dma((16,)), dma((16,)), dma((2, 2, 4)), dma((2, 2, 4)), dma((4, 2, 2)), dma((4, 2, 2)),
         ],
         compiler_params=pltpu.CompilerParams(

time: 159 us -> 148 us (0.931); the launches traced: 157 us -> 148 us
  Pallas kernels: 151 us -> 142 us
    pallas_call x1, Pallas kernels: 151 us -> 142 us  [fused_call(): pl.pallas_call(fused_kernel, in_specs=[smem] * 2 + [vmem] * 4 + [hbm] * 2...]
where the time goes in v5:
time: 148 us
  Pallas kernels  142 us (96%)
  local copies, waits for them, and re-layouts  5.17 us (3%)
    pallas_call x1, Pallas kernels, fused_call(): pl.pallas_call(fused_kernel, in_specs=[smem] * 2 + [vmem] * 4 + [hbm] * 2...  142 us
    unnamed x10, local copies, waits for them, and re-layouts  5.17 us

profile of v5, /device:TPU:0, one launch (start us, length us, event | category | flops | bytes accessed | tf_op | source)
XLA Modules:
  0.0 148.1 jit_solution(5253268635151228518)
XLA Ops:
  0.6 142.3 %exchange.1 = (bf16[128,8192]{1,0:T(8,128)(2,1)}, f32[4,48,512]{2,1,0:T(8,128)}, f32[4,16,256]{2,1,0:T(8,128)}, f32[4,32,128]{2,1,0:T(8,128)}) custom-call(s32[2]{0:T(128)} %tenant_ref.1, s32[2,4]{1,0:T(2,128)} %doc_ref.1, bf16[2048,256]{1,0:T(8,128)(2,1)} %q_ref.1, bf16[2048,128]{1,0:T(8,128)(2,1)} %k_ref.1, bf16[2048,128]{1,0:T(8,128)(2,1)} %v_ref.1, ...), custom_call_target="tpu_custom_call" | custom-call | flops 20000000000 | bytes 40000000 | tf_op jit(solution)/shard_map/exchange/pallas_call | solution.py:785
  142.9 0.0 copy-start
  142.9 0.0 copy-start.2
  142.9 0.0 copy-start.1
  143.0 3.1 %copy.23 = bf16[128,8192]{1,0:T(8,128)(2,1)} copy(bf16[128,8192]{1,0:T(8,128)(2,1)} %get-tuple-element.8) | data formatting | bytes 4194304
  146.1 0.0 copy-done
  146.1 0.7 copy.24
  146.9 0.0 copy-done.2
  146.9 0.6 copy.25
  147.5 0.0 copy-done.1
  147.5 0.6 copy.26
Async XLA Ops:
  142.9 3.2 %copy-start = (f32[4,48,512]{2,1,0:T(8,128)S(1)}, f32[4,48,512]{2,1,0:T(8,128)}, u32[]{:S(2)}) copy-start(f32[4,48,512]{2,1,0:T(8,128)} %get-tuple-element.9) | copy-start | bytes 1179652
  142.9 3.9 %copy-start.2 = (f32[4,16,256]{2,1,0:T(8,128)S(1)}, f32[4,16,256]{2,1,0:T(8,128)}, u32[]{:S(2)}) copy-start(f32[4,16,256]{2,1,0:T(8,128)} %get-tuple-element.10) | copy-start | bytes 196612
  142.9 4.5 %copy-start.1 = (f32[4,32,128]{2,1,0:T(8,128)S(1)}, f32[4,32,128]{2,1,0:T(8,128)}, u32[]{:S(2)}) copy-start(f32[4,32,128]{2,1,0:T(8,128)} %get-tuple-element.11) | copy-start | bytes 196612

commit v6 on v5

--- a/solution.py
+++ b/solution.py
@@ -354,9 +354,17 @@
                 for j in range(1, 4):
                     begin = jnp.where(p_row >= starts[j], starts[j], begin)
                 k_idx = lax.broadcasted_iota(jnp.int32, (width, ROWS), 0)
-                allowed = (k_idx >= begin) & (k_idx <= p_row)
-                st = lax.dot_general(k_ref[keys, :], q, NT, preferred_element_type=F32)
-                st = jnp.where(allowed, st * scale2, MASKED)
+                st = lax.dot_general(k_ref[keys, :], q, NT, preferred_element_type=F32) * scale2
+                far_keys = width - ROWS
+                near_keys = k_idx[far_keys:]
+                masked = jnp.where(
+                    (near_keys >= begin) & (near_keys <= p_row), st[far_keys:], MASKED
+                )
+                if far_keys:
+                    masked = jnp.concatenate(
+                        [jnp.where(k_idx[:far_keys] >= begin, st[:far_keys], MASKED), masked], axis=0
+                    )
+                st = masked
                 top = jnp.max(st, axis=0, keepdims=True)
                 e = jnp.exp2(st - top)
                 inv = 1.0 / jnp.sum(e, axis=0, keepdims=True)
@@ -391,6 +399,10 @@
                         start(outgoing[3 * n : 3 * n + 3])
                         relayed[4 * n].start()
 
+                @pl.when(turn == 1)
+                def _():
+                    arrive(0)
+
         dk = dk_ref[...] * scale
         dk = dk * c_ref[...] + pltpu.roll(dk, HD // 2, 1) * s_ref[...]
         for n, value in enumerate((dk.astype(BF16), dv_ref[...].astype(BF16))):
@@ -419,6 +431,7 @@
         @pl.when(turn == 0)
         def _():
             start(gather_out(0))
+            start(gather_out(3))
             w_own[3].wait()
             w_own[4].wait()
             lowx[x] = lax.dot_general(
@@ -704,8 +717,6 @@
         for copy in forward_in(c):
             copy.wait_recv()
 
-    arrive(0)
-    start(gather_out(3))
     incoming = weights_y(False)
     relayed = weights_core(True)
     for n in range(4):
@@ -756,6 +767,9 @@
     step_output()
     deliver(0)
     step_squares()
+    finish(1)
+    step_update()
+    sq_sent()
     for c in range(8):
         for copy in gather_out(c) + forward_out(c):
             copy.wait_send()
@@ -768,9 +782,6 @@
             copy.wait_send()
     kv_copy.wait_send()
     all_sent(0)
-    step_update()
-    sq_sent()
-    finish(1)
     deliver(1)
     all_sent(1)
 

time: 148 us -> 144 us (0.973)
  Pallas kernels: 142 us -> 138 us
    pallas_call x1, Pallas kernels: 142 us -> 138 us  [fused_call(): pl.pallas_call(fused_kernel, in_specs=[smem] * 2 + [vmem] * 4 + [hbm] * 2...]
where the time goes in v6:
time: 144 us
  Pallas kernels  138 us (96%)
  local copies, waits for them, and re-layouts  5.17 us (4%)
    pallas_call x1, Pallas kernels, fused_call(): pl.pallas_call(fused_kernel, in_specs=[smem] * 2 + [vmem] * 4 + [hbm] * 2...  138 us
    unnamed x10, local copies, waits for them, and re-layouts  5.17 us

profile of v6, /device:TPU:0, one launch (start us, length us, event | category | flops | bytes accessed | tf_op | source)
XLA Modules:
  0.0 143.7 jit_solution(12057698079741730686)
XLA Ops:
  0.6 137.9 %exchange.1 = (bf16[128,8192]{1,0:T(8,128)(2,1)}, f32[4,48,512]{2,1,0:T(8,128)}, f32[4,16,256]{2,1,0:T(8,128)}, f32[4,32,128]{2,1,0:T(8,128)}) custom-call(s32[2]{0:T(128)} %tenant_ref.1, s32[2,4]{1,0:T(2,128)} %doc_ref.1, bf16[2048,256]{1,0:T(8,128)(2,1)} %q_ref.1, bf16[2048,128]{1,0:T(8,128)(2,1)} %k_ref.1, bf16[2048,128]{1,0:T(8,128)(2,1)} %v_ref.1, ...), custom_call_target="tpu_custom_call" | custom-call | flops 20000000000 | bytes 40000000 | tf_op jit(solution)/shard_map/exchange/pallas_call | solution.py:796
  138.5 0.0 copy-start
  138.5 0.0 copy-start.2
  138.5 0.0 copy-start.1
  138.5 3.1 %copy.23 = bf16[128,8192]{1,0:T(8,128)(2,1)} copy(bf16[128,8192]{1,0:T(8,128)(2,1)} %get-tuple-element.8) | data formatting | bytes 4194304
  141.7 0.0 copy-done
  141.7 0.7 copy.24
  142.4 0.0 copy-done.2
  142.4 0.6 copy.25
  143.1 0.0 copy-done.1
  143.1 0.6 copy.26
Async XLA Ops:
  138.5 3.2 %copy-start = (f32[4,48,512]{2,1,0:T(8,128)S(1)}, f32[4,48,512]{2,1,0:T(8,128)}, u32[]{:S(2)}) copy-start(f32[4,48,512]{2,1,0:T(8,128)} %get-tuple-element.9) | copy-start | bytes 1179652
  138.5 3.9 %copy-start.2 = (f32[4,16,256]{2,1,0:T(8,128)S(1)}, f32[4,16,256]{2,1,0:T(8,128)}, u32[]{:S(2)}) copy-start(f32[4,16,256]{2,1,0:T(8,128)} %get-tuple-element.10) | copy-start | bytes 196612
  138.5 4.5 %copy-start.1 = (f32[4,32,128]{2,1,0:T(8,128)S(1)}, f32[4,32,128]{2,1,0:T(8,128)}, u32[]{:S(2)}) copy-start(f32[4,32,128]{2,1,0:T(8,128)} %get-tuple-element.11) | copy-start | bytes 196612

commit v7 on v6

--- a/solution.py
+++ b/solution.py
@@ -201,6 +201,15 @@
     def start(copies):
         for copy in copies:
             copy.start()
+
+    def beside(first):
+        @pl.when(z % 2 == 0)
+        def _():
+            start(gather_out(2 if first else 1))
+
+        @pl.when(z % 2 == 1)
+        def _():
+            start(gather_out(1 if first else 2))
 
     def arrive(c):
         for copy in gather_in(c):
@@ -431,7 +440,7 @@
         @pl.when(turn == 0)
         def _():
             start(gather_out(0))
-            start(gather_out(3))
+            beside(True)
             w_own[3].wait()
             w_own[4].wait()
             lowx[x] = lax.dot_general(
@@ -443,8 +452,8 @@
 
     lax.fori_loop(0, 2, sequence, 0)
 
-    start(gather_out(1))
-    start(gather_out(2))
+    beside(False)
+    start(gather_out(3))
     lowx_recv()
     lowz_start()
     lowall[z] = lowx[...]

time: 144 us -> 144 us (level)
  no operation moved by 1% of the time
where the time goes in v7:
time: 144 us
  Pallas kernels  138 us (96%)
  local copies, waits for them, and re-layouts  5.17 us (4%)
    pallas_call x1, Pallas kernels, fused_call(): pl.pallas_call(fused_kernel, in_specs=[smem] * 2 + [vmem] * 4 + [hbm] * 2...  138 us
    unnamed x10, local copies, waits for them, and re-layouts  5.17 us

profile of v7, /device:TPU:0, one launch (start us, length us, event | category | flops | bytes accessed | tf_op | source)
XLA Modules:
  0.0 143.7 jit_solution(9006398473005004876)
XLA Ops:
  0.6 137.9 %exchange.1 = (bf16[128,8192]{1,0:T(8,128)(2,1)}, f32[4,48,512]{2,1,0:T(8,128)}, f32[4,16,256]{2,1,0:T(8,128)}, f32[4,32,128]{2,1,0:T(8,128)}) custom-call(s32[2]{0:T(128)} %tenant_ref.1, s32[2,4]{1,0:T(2,128)} %doc_ref.1, bf16[2048,256]{1,0:T(8,128)(2,1)} %q_ref.1, bf16[2048,128]{1,0:T(8,128)(2,1)} %k_ref.1, bf16[2048,128]{1,0:T(8,128)(2,1)} %v_ref.1, ...), custom_call_target="tpu_custom_call" | custom-call | flops 20000000000 | bytes 40000000 | tf_op jit(solution)/shard_map/exchange/pallas_call | solution.py:805
  138.5 0.0 copy-start
  138.5 0.0 copy-start.2
  138.5 0.0 copy-start.1
  138.5 3.1 %copy.23 = bf16[128,8192]{1,0:T(8,128)(2,1)} copy(bf16[128,8192]{1,0:T(8,128)(2,1)} %get-tuple-element.8) | data formatting | bytes 4194304
  141.7 0.0 copy-done
  141.7 0.7 copy.24
  142.4 0.0 copy-done.2
  142.4 0.6 copy.25
  143.1 0.0 copy-done.1
  143.1 0.6 copy.26
Async XLA Ops:
  138.5 3.2 %copy-start = (f32[4,48,512]{2,1,0:T(8,128)S(1)}, f32[4,48,512]{2,1,0:T(8,128)}, u32[]{:S(2)}) copy-start(f32[4,48,512]{2,1,0:T(8,128)} %get-tuple-element.9) | copy-start | bytes 1179652
  138.5 3.9 %copy-start.2 = (f32[4,16,256]{2,1,0:T(8,128)S(1)}, f32[4,16,256]{2,1,0:T(8,128)}, u32[]{:S(2)}) copy-start(f32[4,16,256]{2,1,0:T(8,128)} %get-tuple-element.10) | copy-start | bytes 196612
  138.5 4.5 %copy-start.1 = (f32[4,32,128]{2,1,0:T(8,128)S(1)}, f32[4,32,128]{2,1,0:T(8,128)}, u32[]{:S(2)}) copy-start(f32[4,32,128]{2,1,0:T(8,128)} %get-tuple-element.11) | copy-start | bytes 196612
